TPU v7x, 512 devices: a whole 4x8x8 slice. The times are simulated.
512 devices in a mesh: dp: 32 (over y, x_lo, core), panel: 16 (over z, x_hi).
Axes of the slice: x: 4 (x_hi: 2, x_lo: 2; x = x_hi * 2 + x_lo), y: 8, z: 8, core: 2. Of those that a mesh axis runs over, the one named last changes fastest.
Arguments:
- out_grads: bfloat16 [6144, 8256], P('dp', 'panel'), may hold values from -6 to 6
- layer_inputs: bfloat16 [6144, 2048], P('dp'), may hold values from -0.4375 to 0.4375
- query_grads: bfloat16 [512, 8256], P('dp', 'panel'), may hold values from -6 to 6
- query_inputs: bfloat16 [512, 2048], P('dp'), may hold values from -0.25 to 0.25
- basis_out: bfloat16 [8256, 8256], P('panel', 'dp'), may hold values from -0.125 to 0.125
- basis_in: bfloat16 [2048, 2048], P(None, 'panel'), may hold values from -0.125 to 0.125
Outputs:
- eigen_values: float32 [8256, 2048], P('dp', 'panel')
- preconditioned: bfloat16 [8256, 2048], P('dp', 'panel')
All inputs are finite; a program needn't handle non-finite values.
Results may differ from a plain program's by a relative error of at most 0.033.
Values may be sent and summed in bfloat16 or wider, within the bound.
A program may use at most 64 MiB of HBM per device.

v0:
```python
import jax
import jax.numpy as jnp
from jax import lax
from jax.sharding import PartitionSpec as P

damping = 0.1


def per_device(out_grads, layer_inputs, query_grads, query_inputs, basis_out, basis_in):
    in_rot = jnp.dot(layer_inputs, basis_in, preferred_element_type=jnp.float32).astype(
        jnp.bfloat16
    )
    query_in_rot = jnp.dot(query_inputs, basis_in, preferred_element_type=jnp.float32).astype(
        jnp.bfloat16
    )
    all_grads, all_query, all_inputs, all_query_in = (
        lax.all_gather(out_grads, "dp", axis=0, tiled=True),
        lax.all_gather(query_grads, "dp", axis=0, tiled=True),
        lax.all_gather(in_rot, "dp", axis=0, tiled=True),
        lax.all_gather(query_in_rot, "dp", axis=0, tiled=True),
    )
    part_fit = jnp.dot(all_grads, basis_out, preferred_element_type=jnp.float32)
    part_query = jnp.dot(all_query, basis_out, preferred_element_type=jnp.float32)
    sum_fit, sum_query = (
        lax.psum(part_fit.astype(jnp.bfloat16), "panel").astype(jnp.float32),
        lax.psum(part_query.astype(jnp.bfloat16), "panel").astype(jnp.float32),
    )
    fit_rot = sum_fit.astype(jnp.bfloat16)
    query_rot = sum_query.astype(jnp.bfloat16)
    seq_count = lax.axis_size("dp")
    seq_len = out_grads.shape[0]
    per_sequence = jnp.einsum(
        "nsc,nse->nce",
        fit_rot.reshape(seq_count, seq_len, fit_rot.shape[1]),
        all_inputs.reshape(seq_count, seq_len, all_inputs.shape[1]),
        preferred_element_type=jnp.float32,
    )
    eigen_values = jnp.sum(per_sequence * per_sequence, axis=0) / seq_count
    query_sum = jnp.dot(query_rot.T, all_query_in, preferred_element_type=jnp.float32)
    scaled = (query_sum / (eigen_values + damping)).astype(jnp.bfloat16)
    width_in = basis_in.shape[1]
    image_total = lax.psum(
        jnp.dot(basis_in, scaled.T, preferred_element_type=jnp.float32).astype(jnp.bfloat16),
        "panel",
    ).astype(jnp.float32)
    image_mine = lax.dynamic_slice_in_dim(
        image_total, lax.axis_index("panel") * width_in, width_in, 0
    )
    image_block = image_mine.astype(jnp.bfloat16)
    partial_out = jnp.dot(
        lax.all_gather(basis_out, "panel", axis=0, tiled=True),
        image_block.T,
        preferred_element_type=jnp.float32,
    )
    preconditioned = lax.psum_scatter(
        partial_out.astype(jnp.bfloat16), "dp", scatter_dimension=0, tiled=True
    )
    return (eigen_values, preconditioned)


def solution(mesh):
    in_specs = (
        P("dp", "panel"),
        P("dp", None),
        P("dp", "panel"),
        P("dp", None),
        P("panel", "dp"),
        P(None, "panel"),
    )
    out_specs = (P("dp", "panel"), P("dp", "panel"))
    return jax.shard_map(
        per_device, mesh=mesh, in_specs=in_specs, out_specs=out_specs, check_vma=False
    )
```

profile of v0, /device:TPU:6, one launch (start us, length us, event | category | flops | bytes accessed | tf_op | source)
XLA Modules:
  0.0 761.9 jit_solution(7282812074161431916)
XLA Ops:
  7.2 0.0 copy-start
  7.2 0.0 all-gather.5.cloned.1.call-start
  7.2 0.7 all-gather.5.cloned.1.call-update
  7.9 0.0 all-gather.7.cloned.1.call-start
  8.0 0.3 copy-done
  8.3 2.0 convolution_convert_fusion.4
  10.3 0.0 all-gather.7.cloned.1.call-update
  10.3 0.0 all-reduce.8.cloned.1.call-start
  10.4 34.3 %all_gather.17 = bf16[512,516]{1,0:T(8,128)(2,1)S(1)} all-gather(bf16[16,516]{1,0:T(8,128)(2,1)} %param.8), channel_id=1, replica_groups=mesh['dp'=32,'panel'=16] {'dp'}, dimensions={0}, use_global_device_ids=true | all-gather | bytes 544896 | tf_op jit(solution)/shard_map/all_gather | solution.py:18
  44.7 2.1 convolution_convert_fusion.3
  46.8 42.3 %all-gather.5.cloned.1.call-done = bf16[6144,516]{1,0:T(8,128)(2,1)} async-done(((bf16[192,516]{1,0:T(8,128)(2,1)}), bf16[6144,516]{1,0:T(8,128)(2,1)}) %all-gather.5.cloned.1.call-update) | async-done | bytes 6340624 | tf_op jit(solution)/shard_map/all_gather | solution.py:17
  89.1 7.8 %convolution_convert_fusion.1 = bf16[6144,258]{0,1:T(8,128)(2,1)} fusion(bf16[6144,516]{1,0:T(8,128)(2,1)} %all-gather.5.cloned.1.call-done, bf16[516,258]{0,1:T(8,128)(2,1)} %param.10), kind=kOutput, calls=%fused_computation.2 | convolution fusion | flops 1637462016 | bytes 9777168 | tf_op jit(solution)/shard_map/dot_general | solution.py:22
  96.8 8.1 %reshape.10 = bf16[32,192,258]{1,0,2:T(8,128)(2,1)} reshape(bf16[6144,258]{0,1:T(8,128)(2,1)} %convolution_convert_fusion.1) | data formatting | bytes 6340608 | tf_op jit(solution)/shard_map/reshape | solution.py:34
  104.9 6.7 copy.11
  111.6 0.0 copy-start.1
  111.6 0.0 copy-start.4
  111.6 0.0 all-reduce.8.cloned.1.call-update
  111.7 0.0 all-gather.9.cloned.1.call-start
  111.7 0.5 all-gather.9.cloned.1.call-update
  112.2 0.0 all-reduce.6.cloned.1.call-start
  112.3 0.4 copy-done.1
  112.7 0.0 copy-done.4
  112.7 0.2 convolution_convert_fusion.5
  112.9 32.3 %all_gather.18 = bf16[512,128]{1,0:T(8,128)(2,1)S(1)} all-gather(bf16[16,128]{1,0:T(8,128)(2,1)S(1)} %convolution_convert_fusion.5), channel_id=1, replica_groups=mesh['dp'=32,'panel'=16] {'dp'}, dimensions={0}, use_global_device_ids=true | all-gather | bytes 135168 | tf_op jit(solution)/shard_map/all_gather | solution.py:20
  145.2 13.1 %all-gather.7.cloned.1.call-done = bf16[6144,128]{1,0:T(8,128)(2,1)} async-done(((bf16[192,128]{1,0:T(8,128)(2,1)}), bf16[6144,128]{1,0:T(8,128)(2,1)}) %all-gather.7.cloned.1.call-update) | async-done | bytes 1572880 | tf_op jit(solution)/shard_map/all_gather | solution.py:19
  158.3 232.9 %all-reduce.8.cloned.1.call-done = (bf16[32,192,258]{1,2,0:T(8,128)(2,1)}, bf16[512,258]{0,1:T(8,128)(2,1)}) async-done(((bf16[32,192,258]{1,2,0:T(8,128)(2,1)}, bf16[512,258]{0,1:T(8,128)(2,1)}), (bf16[32,192,258]{1,2,0:T(8,128)(2,1)}, bf16[512,258]{0,1:T(8,128)(2,1)})) %all-reduce.8.cloned.1.call-update) | async-done | bytes 3434512 | tf_op jit(solution)/shard_map/psum | solution.py:25
  391.2 0.0 copy-start.3
  391.2 4.0 multiply_reduce_fusion
  395.3 0.0 copy-start.2
  395.3 0.0 copy-done.3
  395.3 1.7 fusion.2
  397.0 0.0 all-reduce.6.cloned.1.call-update
  397.1 111.1 %all-gather.9.cloned.1.call-done = bf16[16,516,258]{1,2,0:T(8,128)(2,1)} async-done(((bf16[1,516,258]{1,2,0:T(8,128)(2,1)}), bf16[16,516,258]{1,2,0:T(8,128)(2,1)}) %all-gather.9.cloned.1.call-update) | async-done | bytes 4260112 | tf_op jit(solution)/shard_map/all_gather | solution.py:51
  508.2 5.6 copy.12
  513.8 0.0 copy-done.2
  513.8 9.1 %reshape.13 = bf16[8256,258]{0,1:T(8,128)(2,1)} reshape(bf16[16,516,258]{1,0,2:T(8,128)(2,1)} %copy.12) | data formatting | bytes 8520192
  522.9 152.2 %all-reduce.6.cloned.1.call-done = bf16[2048,258]{0,1:T(8,128)(2,1)} async-done(((bf16[2048,258]{0,1:T(8,128)(2,1)}), bf16[2048,258]{0,1:T(8,128)(2,1)}) %all-reduce.6.cloned.1.call-update) | async-done | bytes 1056784 | tf_op jit(solution)/shard_map/psum | solution.py:42
  675.1 4.9 fusion.1
  679.9 64.4 %fusion = bf16[272,128]{1,0:T(8,128)(2,1)S(1)} fusion(bf16[8256,128]{1,0:T(8,128)(2,1)S(1)} %fusion.1), kind=kCustom, calls=%all-reduce-scatter | all-reduce-scatter fusion | flops 1114113 | bytes 2185216
  744.3 1.9 collective-permute-start
  746.3 1.9 collective-permute-start.1
  748.2 1.3 dynamic-slice.4
  750.1 3.7 collective-permute-done.1
  753.9 0.0 collective-permute-done
  753.9 0.8 concatenate
  754.7 0.7 constant_dynamic-slice_fusion
  (2 shorter events, 0.0 us)
Async XLA Ops:
  7.2 1.1 copy-start
  7.2 81.9 %all-gather.5.cloned.1.call-start = ((), (), s32[]{:S(2)}) async-start(), calls=%async_computation | async-start | bytes 8110080 | tf_op jit(solution)/shard_map/all_gather | solution.py:17
  7.9 150.4 %all-gather.7.cloned.1.call-start = ((), (), s32[]{:S(2)}) async-start(), calls=%async_computation.1 | async-start | bytes 1622016 | tf_op jit(solution)/shard_map/all_gather | solution.py:19
  10.3 380.9 %all-reduce.8.cloned.1.call-start = ((), (), s32[]{:S(2)}) async-start(), calls=%async_computation.4 | async-start | bytes 9191424 | tf_op jit(solution)/shard_map/psum | solution.py:25
  111.6 1.0 copy-start.1
  111.6 1.0 copy-start.4
  111.7 396.5 %all-gather.9.cloned.1.call-start = ((), (), s32[]{:S(2)}) async-start(), calls=%async_computation.3 | async-start | bytes 5744640 | tf_op jit(solution)/shard_map/all_gather | solution.py:51
  112.2 562.8 %all-reduce.6.cloned.1.call-start = ((), (), s32[]{:S(2)}) async-start(), calls=%async_computation.2 | async-start | bytes 2162688 | tf_op jit(solution)/shard_map/psum | solution.py:42
  391.2 4.1 copy-start.3
  395.3 118.5 %copy-start.2 = (f32[258,128]{1,0:T(8,128)}, f32[258,128]{1,0:T(8,128)S(1)}, u32[]{:S(2)}) copy-start(f32[258,128]{1,0:T(8,128)S(1)} %broadcast_multiply_fusion) | copy-start | bytes 396292
  744.3 9.6 %collective-permute-start = (bf16[272,128]{1,0:T(8,128)(2,1)S(1)}, bf16[272,128]{1,0:T(8,128)(2,1)S(1)}, u32[]{:S(2)}, u32[]{:S(2)}) collective-permute-start(bf16[272,128]{1,0:T(8,128)(2,1)S(1)} %fusion), channel_id=1, source_target_pairs={{0,16},{16,32},{32,48},{48,64},{64,80},{80,96},{96,112},{112,128},... | collective-permute-start | bytes 208904
  746.3 7.6 collective-permute-start.1
Sparse Core Ops, SparseCore 0:
  10.2 78.8 all-gather.4
  91.8 66.4 all-gather.6
  161.4 229.8 all-reduce.7
  394.3 113.8 all-gather.8
  511.0 164.0 all-reduce.5
where the time goes:
time: 766 us; the launch traced here: 762 us
  waiting for transfers between devices  557 us (73%)
  blocking collectives  131 us (17%)
  local copies, waits for them, and re-layouts  32.9 us (4%)
  matrix products  22.7 us (3%)
  between operations  14.5 us (2%)
    psum x1, waiting for transfers between devices, per_device(): lax.psum(part_fit.astype(jnp.bfloat16), 'panel').astype(jnp.float32)  233 us
    psum x1, waiting for transfers between devices, per_device(): lax.psum(jnp.dot(basis_in, scaled.T, preferred_element_type=jnp.float32)....  152 us
    all_gather x1, waiting for transfers between devices, per_device(): lax.all_gather(basis_out, 'panel', axis=0, tiled=True)  111 us
    unnamed x1, blocking collectives  64.4 us
    all_gather x1, waiting for transfers between devices, per_device(): lax.all_gather(out_grads, 'dp', axis=0, tiled=True)  42.3 us
    all_gather x1, blocking collectives, per_device(): lax.all_gather(query_grads, 'dp', axis=0, tiled=True)  34.3 us
    all_gather x1, blocking collectives, per_device(): lax.all_gather(query_in_rot, 'dp', axis=0, tiled=True)  32.3 us
  transfers between devices with their start and end apart: 7, of which 6 were waited for; matrix products, arithmetic and copies ran while one was open for 6% of the time, Pallas kernels for 0%

commit v1 on v0

v1 whole, which is shorter than its diff:
```python
import functools

import jax
import jax.numpy as jnp
from jax import lax
from jax.experimental import pallas as pl
from jax.experimental.pallas import tpu as pltpu
from jax.sharding import PartitionSpec as P

damping = 0.1
bf16 = jnp.bfloat16
f32 = jnp.float32
SEQ = 192
TOK = 208
COL = 258
PAD = 272
MAIN = 512
N_SEQ = 32
RING = 8
NT = (((1,), (1,)), ((), ()))


def coords():
    dp, panel = lax.axis_index("dp"), lax.axis_index("panel")
    y, xl, c = lax.div(dp, 4), lax.rem(lax.div(dp, 2), 2), lax.rem(dp, 2)
    return y, xl, c, lax.div(panel, 2), lax.rem(panel, 2)


def device(y, xl, c, z, xh):
    return (y * 4 + xl * 2 + c, z * 2 + xh)


def turn(pos, by):
    return lax.rem(pos + by + RING, RING)


def x_device(x, y, c, z):
    x = lax.rem(x + 4, 4)
    return device(y, lax.rem(x, 2), c, z, lax.div(x, 2))


def signal(who):
    pl.semaphore_signal(
        pltpu.get_barrier_semaphore(), inc=1, device_id=who, device_id_type=pl.DeviceIdType.MESH
    )


def wait_all(count):
    pl.semaphore_wait(pltpu.get_barrier_semaphore(), count)


class Copies:
    def __init__(self, send, recv):
        self.send, self.recv, self.used, self.started = send, recv, 0, []

    def make(self, src, dst, who):
        k = self.used
        self.used += 1
        return pltpu.make_async_remote_copy(
            src_ref=src, dst_ref=dst, send_sem=self.send.at[k], recv_sem=self.recv.at[k],
            device_id=who, device_id_type=pl.DeviceIdType.MESH,
        )

    def start(self, src, dst, who):
        copy = self.make(src, dst, who)
        copy.start()
        self.started.append(copy)
        return copy

    def finish(self):
        for copy in self.started:
            copy.wait_send()


def permute(copies, local_sem, src, dst, who, same):
    copy = copies.make(src, dst, who)
    local = pltpu.make_async_copy(src, dst, local_sem)

    @pl.when(jnp.logical_not(same))
    def _():
        copy.start()

    @pl.when(same)
    def _():
        local.start()

    def wait():
        @pl.when(jnp.logical_not(same))
        def _():
            copy.wait()

        @pl.when(same)
        def _():
            local.wait()

    return wait


def gather_ring(copies, pos, up, down, slot, ready=None):
    ups = copies.start(slot(pos), slot(pos), up)
    downs = copies.start(slot(pos), slot(pos), down)
    if ready is not None:
        ready(pos)
    for t in range(1, 5):
        at = turn(pos, -t)
        ups.wait_recv()
        if t < 4:
            ups = copies.start(slot(at), slot(at), up)
        if ready is not None:
            ready(at)
        if t < 4:
            at = turn(pos, t)
            downs.wait_recv()
            if t < 3:
                downs = copies.start(slot(at), slot(at), down)
            if ready is not None:
                ready(at)


def scatter_ring(copies, pos, up, down, chunk, sent, got):
    ups = downs = None
    for t in range(4):
        value = chunk(turn(pos, 4 - t))
        if t:
            ups.wait_recv()
        for a, part in enumerate(value):
            total = part + got[t - 1, a].astype(f32) if t else part
            sent[t, a] = total.astype(bf16)
        ups = copies.start(sent.at[t], got.at[t], up)
        if t < 3:
            value = chunk(turn(pos, t - 3))
            if t:
                downs.wait_recv()
            for a, part in enumerate(value):
                total = part + got[3 + t, a].astype(f32) if t else part
                sent[4 + t, a] = total.astype(bf16)
            downs = copies.start(sent.at[4 + t], got.at[4 + t], down)
    value = chunk(pos)
    ups.wait_recv()
    downs.wait_recv()
    return [
        part + got[3, a].astype(f32) + got[6, a].astype(f32) for a, part in enumerate(value)
    ]


def gather_kernel(gm, gt, f, bm, bt, gm_out, gt_out, f_out, bm_out, bt_out, send, recv, local):
    y, xl, c, z, xh = coords()
    x = xh * 2 + xl
    other = device(y, xl, 1 - c, z, xh)
    up, down = device(turn(y, 1), xl, c, z, xh), device(turn(y, -1), xl, c, z, xh)
    right, left = x_device(x + 1, y, c, z), x_device(x + 3, y, c, z)
    pair = device(y, 1 - xl, c, z, xh)
    g_to, g_from = device(y, c, xh, z, xl), device(y, xh, xl, z, c)
    g_same = jnp.logical_and(xh == xl, xl == c)
    f_to = device(z, xh, c, y, xl)
    f_same = jnp.logical_and(y == z, xl == xh)

    for who in (other, up, down, right, left):
        signal(who)

    @pl.when(jnp.logical_not(g_same))
    def _():
        signal(g_from)

    @pl.when(jnp.logical_not(f_same))
    def _():
        signal(f_to)

    wait_all(7 - g_same.astype(jnp.int32) - f_same.astype(jnp.int32))

    copies = Copies(send, recv)
    g_wait = permute(copies, local.at[0], gm, gm_out.at[xh, y], g_to, g_same)
    t_wait = permute(copies, local.at[1], gt, gt_out.at[y, xh], g_to, g_same)
    f_wait = permute(copies, local.at[2], f, f_out.at[c, z, xh], f_to, f_same)

    own_m = pltpu.make_async_copy(bm, bm_out.at[x], local.at[3])
    own_t = pltpu.make_async_copy(bt, bt_out.at[x], local.at[4])
    own_m.start()
    own_t.start()
    m_right = copies.start(bm, bm_out.at[x], right)
    m_left = copies.start(bm, bm_out.at[x], left)
    t_right = copies.start(bt, bt_out.at[x], right)
    t_left = copies.start(bt, bt_out.at[x], left)

    g_wait()
    t_wait()
    forwards = []

    def pass_on(ref):
        def ready(at):
            forwards.append(copies.start(ref(at), ref(at), other))

        return ready

    def slots_g(at):
        return gm_out.at[c, at]

    def slots_t(at):
        return gt_out.at[at, c]

    def slots_f(at):
        return f_out.at[c, at]

    f_wait()
    swapped = copies.start(f_out.at[c, y, xl], f_out.at[c, y, xl], pair)
    gather_ring(copies, y, up, down, slots_g, pass_on(slots_g))
    x_l, x_r = lax.rem(x + 3, 4), lax.rem(x + 1, 4)
    m_right.wait_recv()
    far_a = copies.start(
        bm_out.at[x_l, pl.ds(0, 144)], bm_out.at[x_l, pl.ds(0, 144)], right
    )
    m_left.wait_recv()
    far_b = copies.start(
        bm_out.at[x_r, pl.ds(144, 128)], bm_out.at[x_r, pl.ds(144, 128)], left
    )
    t_right.wait_recv()
    t_left.wait_recv()
    far_t = copies.start(bt_out.at[x_l], bt_out.at[x_l], right)
    gather_ring(copies, y, up, down, slots_t, pass_on(slots_t))
    swapped.wait_recv()
    gather_ring(copies, y, up, down, slots_f, pass_on(slots_f))
    far_a.wait_recv()
    far_b.wait_recv()
    far_t.wait_recv()
    for copy in forwards:
        copy.wait_recv()
    own_m.wait()
    own_t.wait()
    copies.finish()


def rotate_kernel(bm, bt, gm, gt, out, sent, got, stage, landed, send, recv):
    y, xl, c, z, xh = coords()
    up, down = device(y, xl, c, turn(z, 1), xh), device(y, xl, c, turn(z, -1), xh)
    pair = device(y, 1 - xl, c, z, xh)
    for who in (up, down, pair):
        signal(who)
    wait_all(3)
    copies = Copies(send, recv)

    def chunk(d):
        part = lax.dot_general(bm[0], gm[0, d], NT, preferred_element_type=f32)
        part += lax.dot_general(bm[1], gm[1, d], NT, preferred_element_type=f32)
        part += jnp.dot(bt[...], gt[d], preferred_element_type=f32)[:, :TOK]
        return [part]

    (total,) = scatter_ring(copies, z, up, down, chunk, sent, got)
    stage[0] = total[:PAD].astype(bf16)
    stage[1] = total[PAD:].astype(bf16)
    swap = copies.start(stage.at[1 - xl], landed, pair)
    out[xl] = stage[xl]
    swap.wait_recv()
    out[1 - xl] = landed[...]
    copies.finish()


def solve_kernel(
    rot, f, bo, bi, eig, pre,
    lhs, sent_a, got_a, tot_a, stage_a, land_a, s_buf, core_s, core_r,
    sent_b, got_b, tot_b, stage_b, land_b, u_out, u_in,
    sent_c, got_c, tot_c, stage_c, land_c, send, recv, local,
):
    y, xl, c, z, xh = coords()
    other = device(y, xl, 1 - c, z, xh)
    y_up, y_down = device(turn(y, 1), xl, c, z, xh), device(turn(y, -1), xl, c, z, xh)
    z_up, z_down = device(y, xl, c, turn(z, 1), xh), device(y, xl, c, turn(z, -1), xh)
    pair_l, pair_h = device(y, 1 - xl, c, z, xh), device(y, xl, c, z, 1 - xh)
    u_to = device(z, xh, c, y, xl)
    u_same = jnp.logical_and(y == z, xl == xh)
    for who in (other, y_up, y_down, z_up, z_down, pair_l, pair_h):
        signal(who)

    @pl.when(jnp.logical_not(u_same))
    def _():
        signal(u_to)

    wait_all(8 - u_same.astype(jnp.int32))
    copies = Copies(send, recv)

    lane = lax.broadcasted_iota(jnp.int32, (PAD, TOK), 1)
    for h in range(2):
        value = rot[h]
        zero = jnp.zeros_like(value)
        lhs[h, :PAD] = jnp.where(lane < SEQ, value, zero)
        lhs[h, PAD:] = jnp.where(lane < SEQ, zero, value)

    def chunk_a(d):
        parts = []
        for side in range(2):
            first = jnp.dot(lhs[0], f[0, d, side], preferred_element_type=f32)
            second = jnp.dot(lhs[1], f[1, d, side], preferred_element_type=f32)
            parts.append(first[:PAD] * first[:PAD] + second[:PAD] * second[:PAD])
            parts.append(first[PAD:] + second[PAD:])
        return parts

    total = scatter_ring(copies, z, z_up, z_down, chunk_a, sent_a, got_a)
    for a, part in enumerate(total):
        tot_a[a // 2, a % 2] = part
    stage_a[...] = tot_a[1 - xh].astype(bf16)
    swap = copies.start(stage_a, land_a, pair_h)
    swap.wait_recv()
    values = (tot_a[xh, 0] + land_a[0].astype(f32)) / N_SEQ
    sums = tot_a[xh, 1] + land_a[1].astype(f32)
    eig[...] = values[:COL]
    s_buf[z, xh] = (sums / (values + damping)).astype(bf16)

    swap = copies.start(s_buf.at[z, xh], s_buf.at[z, xh], pair_h)
    swap.wait_recv()

    across = []

    def to_core(d):
        for side in range(2):
            core_s[d, side] = jnp.dot(
                bo[1 - c], s_buf[d, side], preferred_element_type=f32
            ).astype(bf16)

    gather_ring(copies, z, z_up, z_down, lambda at: s_buf.at[at])
    order = [turn(y, by) for by in (4, -3, 3, -2, 2, -1, 1, 0)]
    for d in order:
        to_core(d)
        across.append(copies.start(core_s.at[d], core_r.at[d], other))
    waits = iter(across)

    def chunk_b(d):
        parts = [
            jnp.dot(bo[c], s_buf[d, side], preferred_element_type=f32) for side in range(2)
        ]
        next(waits).wait_recv()
        return [part + core_r[d, side].astype(f32) for side, part in enumerate(parts)]

    total = scatter_ring(copies, y, y_up, y_down, chunk_b, sent_b, got_b)
    for a, part in enumerate(total):
        tot_b[a] = part
    stage_b[...] = tot_b[1 - xl].astype(bf16)
    swap = copies.start(stage_b, land_b, pair_l)
    swap.wait_recv()
    u_out[...] = (tot_b[xl] + land_b[...].astype(f32)).astype(bf16)
    permute(copies, local, u_out, u_in, u_to, u_same)()

    def chunk_c(d):
        return [
            lax.dot_general(u_in[...], bi[2 * d + side], NT, preferred_element_type=f32)
            for side in range(2)
        ]

    total = scatter_ring(copies, z, z_up, z_down, chunk_c, sent_c, got_c)
    for a, part in enumerate(total):
        tot_c[a] = part
    stage_c[...] = tot_c[1 - xh].astype(bf16)
    swap = copies.start(stage_c, land_c, pair_h)
    swap.wait_recv()
    pre[...] = (tot_c[xh] + land_c[...].astype(f32))[:COL].astype(bf16)
    copies.finish()


def params(number):
    return pltpu.CompilerParams(
        collective_id=number, has_side_effects=True, vmem_limit_bytes=48 * 2**20
    )


def per_device(out_grads, layer_inputs, query_grads, query_inputs, basis_out, basis_in):
    shape = jax.ShapeDtypeStruct
    anywhere, vmem = pl.BlockSpec(memory_space=pl.ANY), pl.BlockSpec(memory_space=pltpu.VMEM)
    dma = pltpu.SemaphoreType.DMA

    tokens = jnp.concatenate([out_grads, query_grads], axis=0)
    gm = tokens[:, :MAIN]
    gt = jnp.pad(tokens[:, MAIN:].T, ((0, 12), (0, 48)))
    f = jnp.concatenate(
        [
            jnp.dot(layer_inputs, basis_in, preferred_element_type=f32).astype(bf16),
            jnp.dot(query_inputs, basis_in, preferred_element_type=f32).astype(bf16),
        ],
        axis=0,
    )
    bm = jnp.pad(basis_out[:MAIN].T, ((0, PAD - COL), (0, 0)))
    bt = jnp.pad(basis_out[MAIN:], ((0, 12), (0, PAD - COL)))
    gm_all, gt_all, f_all, bm_all, bt_all = pl.pallas_call(
        gather_kernel,
        out_shape=[
            shape((2, RING, TOK, MAIN), bf16),
            shape((RING, 2, 16, 256), bf16),
            shape((2, RING, 2, TOK, 128), bf16),
            shape((4, PAD, MAIN), bf16),
            shape((4, 16, PAD), bf16),
        ],
        in_specs=[anywhere] * 5,
        out_specs=[anywhere] * 5,
        scratch_shapes=[dma((56,)), dma((56,)), dma((5,))],
        compiler_params=params(0),
    )(gm, gt, f, bm, bt)

    tail = bt_all.reshape(2, 2, 16, PAD).transpose(1, 3, 0, 2).reshape(2 * PAD, 32)
    rot = pl.pallas_call(
        rotate_kernel,
        out_shape=shape((2, PAD, TOK), bf16),
        in_specs=[vmem] * 4,
        out_specs=vmem,
        scratch_shapes=[
            pltpu.VMEM((7, 1, 2 * PAD, TOK), bf16),
            pltpu.VMEM((7, 1, 2 * PAD, TOK), bf16),
            pltpu.VMEM((2, PAD, TOK), bf16),
            pltpu.VMEM((PAD, TOK), bf16),
            dma((8,)),
            dma((8,)),
        ],
        compiler_params=params(1),
    )(bm_all.reshape(2, 2 * PAD, MAIN), tail, gm_all, gt_all.reshape(RING, 32, 256))

    bo = jnp.pad(
        basis_out.reshape(2, COL, COL), ((0, 0), (0, PAD - COL), (0, PAD - COL))
    )

    def buffers(parts):
        return [
            pltpu.VMEM((7, parts, PAD, 128), bf16),
            pltpu.VMEM((7, parts, PAD, 128), bf16),
        ]

    return pl.pallas_call(
        solve_kernel,
        out_shape=[shape((COL, 128), f32), shape((COL, 128), bf16)],
        in_specs=[vmem] * 4,
        out_specs=[vmem] * 2,
        scratch_shapes=[
            pltpu.VMEM((2, 2 * PAD, TOK), bf16),
            *buffers(4),
            pltpu.VMEM((2, 2, PAD, 128), f32),
            pltpu.VMEM((2, PAD, 128), bf16),
            pltpu.VMEM((2, PAD, 128), bf16),
            pltpu.VMEM((RING, 2, PAD, 128), bf16),
            pltpu.VMEM((RING, 2, PAD, 128), bf16),
            pltpu.VMEM((RING, 2, PAD, 128), bf16),
            *buffers(2),
            pltpu.VMEM((2, PAD, 128), f32),
            pltpu.VMEM((PAD, 128), bf16),
            pltpu.VMEM((PAD, 128), bf16),
            pltpu.VMEM((PAD, 128), bf16),
            pltpu.VMEM((PAD, 128), bf16),
            *buffers(2),
            pltpu.VMEM((2, PAD, 128), f32),
            pltpu.VMEM((PAD, 128), bf16),
            pltpu.VMEM((PAD, 128), bf16),
            dma((48,)),
            dma((48,)),
            dma,
        ],
        compiler_params=params(2),
    )(rot, f_all, bo, basis_in.reshape(16, 128, 128))


def solution(mesh):
    in_specs = (
        P("dp", "panel"),
        P("dp", None),
        P("dp", "panel"),
        P("dp", None),
        P("panel", "dp"),
        P(None, "panel"),
    )
    out_specs = (P("dp", "panel"), P("dp", "panel"))
    return jax.shard_map(
        per_device, mesh=mesh, in_specs=in_specs, out_specs=out_specs, check_vma=False
    )
```

time: 766 us -> 251 us (0.33)
  waiting for transfers between devices: 557 us -> 0 us
  Pallas kernels: 0 us -> 230 us
  blocking collectives: 131 us -> 0 us
  matrix products: 22.7 us -> 0.53 us
  local copies, waits for them, and re-layouts: 32.9 us -> 16 us
  between operations: 14.5 us -> 0.81 us
    psum x2 -> x0, waiting for transfers between devices: 385 us -> none  [the longest x1 233 us: per_device(): lax.psum(part_fit.astype(jnp.bfloat16), 'panel').astype(jnp.float32)]
    pallas_call x0 -> x3, Pallas kernels: none -> 230 us  [the longest x1 114 us: per_device(): pl.pallas_call(solve_kernel, out_shape=[shape((COL, 128), f32), shape((CO...]
    all_gather x3 -> x0, waiting for transfers between devices: 166 us -> none  [the longest x1 111 us: per_device(): lax.all_gather(basis_out, 'panel', axis=0, tiled=True)]
    all_gather x2 -> x0, blocking collectives: 66.7 us -> none  [the longest x1 34.3 us: per_device(): lax.all_gather(query_grads, 'dp', axis=0, tiled=True)]
    unnamed x1 -> x0, blocking collectives: 64.4 us -> none
    dot_general x7 -> x2, matrix products: 22.7 us -> 0.53 us  [the longest x1 0.35 us: per_device(): jnp.dot(layer_inputs, basis_in, preferred_element_type=f32).astype(bf16)]
    reshape x2 -> x5, local copies, waits for them, and re-layouts: 14.8 us -> 4.61 us  [the longest x2 4.34 us: per_device(): basis_out.reshape(2, COL, COL)]
  transfers between devices with their start and end apart: 7 -> 0, of which waited for: 6 -> 0; matrix products, arithmetic and copies ran while one was open for 6% -> 0% of each run, Pallas kernels for 0% -> 0%
where the time goes in v1:
time: 251 us; the launch traced here: 248 us
  Pallas kernels  230 us (92%)
  local copies, waits for them, and re-layouts  16 us (6%)
    pallas_call x1, Pallas kernels, per_device(): pl.pallas_call(solve_kernel, out_shape=[shape((COL, 128), f32), shape((CO...  114 us
    pallas_call x1, Pallas kernels, per_device(): pl.pallas_call(gather_kernel, out_shape=[shape((2, RING, TOK, MAIN), bf16...  72.8 us
    pallas_call x1, Pallas kernels, per_device(): pl.pallas_call(rotate_kernel, out_shape=shape((2, PAD, TOK), bf16), in_sp...  42.3 us
    unnamed x25, local copies, waits for them, and re-layouts  10.2 us

profile of v1, /device:TPU:6, one launch (start us, length us, event | category | flops | bytes accessed | tf_op | source)
XLA Modules:
  0.0 247.7 jit_solution(17094358974834501993)
XLA Ops:
  0.6 0.0 copy-start
  0.6 0.0 copy-start.8
  0.7 0.0 copy-start.1
  0.7 1.2 copy.14
  1.9 0.8 copy.15
  2.7 0.1 fusion
  2.8 0.0 copy-start.9
  2.9 0.1 copy.17.gm
  3.0 0.1 fusion.1
  3.1 0.0 slice-start
  3.1 0.0 copy-done.8
  3.1 0.0 copy-done
  3.2 0.0 copy-done.1
  3.2 0.4 convolution_convert_fusion
  3.5 0.2 copy-done.9
  3.7 0.2 convolution_convert_fusion.1
  3.9 0.6 pad_maximum_fusion.f
  4.5 0.0 slice-done
  4.5 0.1 copy.21
  4.6 0.0 copy-start.5
  4.6 0.8 copy-done.5
  5.4 72.8 %shard_map.77 = (bf16[2,8,208,512]{3,2,1,0:T(8,128)(2,1)}, bf16[8,2,16,256]{3,2,1,0:T(8,128)(2,1)S(1)}, bf16[2,8,2,208,128]{4,3,2,1,0:T(8,128)(2,1)S(1)}, bf16[4...) custom-call(bf16[208,512]{1,0:T(8,128)(2,1)S(1)} %copy.17.gm, bf16[16,256]{1,0:T(8,128)(2,1)S(1)} %pad.16.gt, ...), custom_call_target="tpu_custom_call" | custom-call | tf_op jit(solution)/shard_map/pallas_call | solution.py:380
  78.3 0.0 copy-start.3
  78.3 1.0 copy-done.3
  79.3 0.0 copy-start.6
  79.3 0.7 copy-done.6
  80.0 0.1 reshape.24
  80.1 0.1 copy.19.bt
  80.2 0.0 copy-start.2
  80.2 2.0 copy-done.2
  82.2 0.0 copy-start.4
  82.2 1.2 copy-done.4
  83.4 0.0 copy-start.7
  83.4 0.9 copy-done.7
  84.3 42.3 %shard_map.78.rot = bf16[2,272,208]{2,1,0:T(8,128)(2,1)S(1)} custom-call(bf16[2,544,512]{2,1,0:T(8,128)(2,1)S(1)} %bitcast.20, bf16[544,32]{1,0:T(8,128)(2,1)S(1)} %copy.19.bt, bf16[2,8,208,512]{3,2,1,0:T(8,128)(2,1)S(1)} %copy-done.2, bf16[8,32,256]{2,1,0:T(8,128)(2,1)S(1)} %bitcast.21), custom_call_target="tpu_custom_call" | custom-call | tf_op jit(solution)/shard_map/pallas_call | solution.py:396
  126.6 2.3 reshape.26
  129.0 2.0 copy.20
  131.0 1.0 pad.19.bo
  132.0 114.4 %shard_map.79 = (f32[258,128]{1,0:T(8,128)S(1)}, bf16[258,128]{1,0:T(8,128)(2,1)S(1)}) custom-call(bf16[2,272,208]{2,1,0:T(8,128)(2,1)S(1)} %shard_map.78.rot, bf16[2,8,2,208,128]{4,3,2,1,0:T(8,128)(2,1)S(1)} %get-tuple-element.11.f, bf16[2,272,272]{2,1,0:T(8,128)(2,1)S(1)} %pad.19.bo, bf16[16,128,128]{2,1,0:T(8,128)(2,1)S(1)} %bitcast.19), custom_call_target="tpu_custom_call" | custom-call | tf_op jit(solution)/shard_map/pallas_call | solution.py:422
  246.4 0.7 copy.26
  247.1 0.6 copy.27
  (5 shorter events, 0.1 us)
Async XLA Ops:
  0.6 2.5 %copy-start = (bf16[192,2048]{1,0:T(8,128)(2,1)S(1)}, bf16[192,2048]{1,0:T(8,128)(2,1)}, u32[]{:S(2)}) copy-start(bf16[192,2048]{1,0:T(8,128)(2,1)} %param.7) | copy-start | bytes 2359300
  0.6 2.4 copy-start.8
  0.7 2.5 %copy-start.1 = (bf16[2048,128]{1,0:T(8,128)(2,1)S(1)}, bf16[2048,128]{1,0:T(8,128)(2,1)}, u32[]{:S(2)}) copy-start(bf16[2048,128]{1,0:T(8,128)(2,1)} %param.11) | copy-start | bytes 1572868
  2.8 0.8 copy-start.9
  3.1 1.4 slice-start
  4.6 0.8 copy-start.5
  78.3 1.0 copy-start.3
  79.3 0.7 copy-start.6
  80.2 2.0 copy-start.2
  82.2 1.2 copy-start.4
  83.4 0.9 copy-start.7

commit v2 on v0

v2 whole, which is shorter than its diff:
```python
import jax
import jax.numpy as jnp
from jax import lax
from jax.experimental import pallas as pl
from jax.experimental.pallas import tpu as pltpu
from jax.sharding import PartitionSpec as P

damping = 0.1
bf16 = jnp.bfloat16
f32 = jnp.float32
SEQ = 192
TOK = 208
COL = 258
PAD = 272
MAIN = 512
N_SEQ = 32
RING = 8
NT = (((1,), (1,)), ((), ()))
TN = (((0,), (0,)), ((), ()))
N_SEM = 256


def coords():
    dp, panel = lax.axis_index("dp"), lax.axis_index("panel")
    y, xl, c = lax.div(dp, 4), lax.rem(lax.div(dp, 2), 2), lax.rem(dp, 2)
    return y, xl, c, lax.div(panel, 2), lax.rem(panel, 2)


def device(y, xl, c, z, xh):
    return (y * 4 + xl * 2 + c, z * 2 + xh)


def turn(pos, by):
    return lax.rem(pos + by + RING, RING)


def x_device(x, y, c, z):
    x = lax.rem(x + 4, 4)
    return device(y, lax.rem(x, 2), c, z, lax.div(x, 2))


def signal(who):
    pl.semaphore_signal(
        pltpu.get_barrier_semaphore(), inc=1, device_id=who, device_id_type=pl.DeviceIdType.MESH
    )


def wait_all(count):
    pl.semaphore_wait(pltpu.get_barrier_semaphore(), count)


class Copies:
    def __init__(self, send, recv):
        self.send, self.recv, self.used, self.started = send, recv, 0, []

    def make(self, src, dst, who):
        k = self.used
        self.used += 1
        return pltpu.make_async_remote_copy(
            src_ref=src, dst_ref=dst, send_sem=self.send.at[k], recv_sem=self.recv.at[k],
            device_id=who, device_id_type=pl.DeviceIdType.MESH,
        )

    def start(self, src, dst, who):
        copy = self.make(src, dst, who)
        copy.start()
        self.started.append(copy)
        return copy

    def finish(self):
        for copy in self.started:
            copy.wait_send()


def permute(copies, local_sem, src, dst, who, same):
    copy = copies.make(src, dst, who)
    local = pltpu.make_async_copy(src, dst, local_sem)

    @pl.when(jnp.logical_not(same))
    def _():
        copy.start()

    @pl.when(same)
    def _():
        local.start()

    def wait():
        @pl.when(jnp.logical_not(same))
        def _():
            copy.wait()

        @pl.when(same)
        def _():
            local.wait()

    return wait


def run(*streams):
    live = list(streams)
    while live:
        for stream in list(live):
            try:
                next(stream)
            except StopIteration:
                live.remove(stream)


def gather_stream(copies, pos, ways, sign, slot, ready=None, first=None):
    ahead, back = ways[::sign]
    if first is not None:
        yield
        first()
    a = copies.start(slot(pos), slot(pos), ahead)
    b = copies.start(slot(pos), slot(pos), back)
    if ready is not None:
        ready(pos)
    for t in range(1, 5):
        yield
        at = turn(pos, -sign * t)
        a.wait_recv()
        if t < 4:
            a = copies.start(slot(at), slot(at), ahead)
        if ready is not None:
            ready(at)
        if t < 4:
            yield
            at = turn(pos, sign * t)
            b.wait_recv()
            if t < 3:
                b = copies.start(slot(at), slot(at), back)
            if ready is not None:
                ready(at)


def scatter_stream(copies, pos, ways, sign, chunk, sent, got, done):
    ahead, back = ways[::sign]
    a = b = None
    for t in range(4):
        value = chunk(turn(pos, sign * (4 - t)))
        if t:
            yield
            a.wait_recv()
            value = value + got[t - 1].astype(f32)
        sent[t] = value.astype(bf16)
        a = copies.start(sent.at[t], got.at[t], ahead)
        if t < 3:
            value = chunk(turn(pos, sign * (t - 3)))
            if t:
                yield
                b.wait_recv()
                value = value + got[3 + t].astype(f32)
            sent[4 + t] = value.astype(bf16)
            b = copies.start(sent.at[4 + t], got.at[4 + t], back)
    value = chunk(pos)
    yield
    a.wait_recv()
    b.wait_recv()
    done(value + got[3].astype(f32) + got[6].astype(f32))


def kernel(
    gm_in, gt_in, f_in, q_in, bm_in, bt_in, bo, bi, eig, pre,
    gm, gt, f, qi, bm, bt, btt, fit_s, fit_g, qry_s, qry_g, stage, landed, stage_q, landed_q,
    rot, qr, sq_s, sq_g, stage_a, landed_a, s_buf, core_s, core_r, u_s, u_g, stage_b, landed_b,
    u_out, u_mine, p_s, p_g, stage_c, landed_c, send, recv, core_send, core_recv, local,
):
    y, xl, c, z, xh = coords()
    x = xh * 2 + xl
    other = device(y, xl, 1 - c, z, xh)
    along_y = (device(turn(y, 1), xl, c, z, xh), device(turn(y, -1), xl, c, z, xh))
    along_z = (device(y, xl, c, turn(z, 1), xh), device(y, xl, c, turn(z, -1), xh))
    right, left = x_device(x + 1, y, c, z), x_device(x + 3, y, c, z)
    pair_l, pair_h = device(y, 1 - xl, c, z, xh), device(y, xl, c, z, 1 - xh)
    g_to, g_from = device(y, c, xh, z, xl), device(y, xh, xl, z, c)
    g_same = jnp.logical_and(xh == xl, xl == c)
    f_to = device(z, xh, c, y, xl)
    f_same = jnp.logical_and(y == z, xl == xh)

    for who in (other, *along_y, *along_z, right, left, pair_h):
        signal(who)

    @pl.when(jnp.logical_not(g_same))
    def _():
        signal(g_from)

    @pl.when(jnp.logical_not(f_same))
    def _():
        signal(f_to)

    wait_all(10 - g_same.astype(jnp.int32) - f_same.astype(jnp.int32))
    copies = Copies(send, recv)

    g_wait = permute(copies, local.at[0], gm_in, gm.at[xh, y], g_to, g_same)
    t_wait = permute(copies, local.at[1], gt_in, gt.at[y, pl.ds(xh * 16, 16)], g_to, g_same)
    f_wait = permute(copies, local.at[2], f_in, f.at[c, z, xh], f_to, f_same)

    def bm_at(q):
        return bm.at[lax.div(q, 2), lax.rem(q, 2)]

    def bt_at(q):
        return bt.at[lax.rem(q, 2), pl.ds(lax.div(q, 2) * 16, 16)]

    own = [
        pltpu.make_async_copy(bm_in, bm_at(x), local.at[3]),
        pltpu.make_async_copy(bt_in, bt_at(x), local.at[4]),
        pltpu.make_async_copy(q_in, qi.at[y, xl, c], local.at[5]),
    ]
    for copy in own:
        copy.start()
    m_right = copies.start(bm_in, bm_at(x), right)
    m_left = copies.start(bm_in, bm_at(x), left)
    t_right = copies.start(bt_in, bt_at(x), right)
    t_left = copies.start(bt_in, bt_at(x), left)
    q_swap = copies.start(q_in, qi.at[y, xl, c], pair_l)

    forwards = []

    def pass_on(slot):
        def ready(at):
            forwards.append(copies.start(slot(at), slot(at), other))

        return ready

    def around(slot, sign, first=None):
        return gather_stream(copies, y, along_y, sign, slot, pass_on(slot), first)

    own[2].wait()
    q_swap.wait_recv()
    g_wait()
    t_wait()
    far = []

    def over_x():
        x_l, x_r = lax.rem(x + 3, 4), lax.rem(x + 1, 4)
        yield
        m_right.wait_recv()
        half = bm_at(x_l).at[pl.ds(0, 144)]
        far.append(copies.start(half, half, right))
        yield
        m_left.wait_recv()
        half = bm_at(x_r).at[pl.ds(144, 128)]
        far.append(copies.start(half, half, left))
        t_right.wait_recv()
        t_left.wait_recv()
        far.append(copies.start(bt_at(x_l), bt_at(x_l), right))

    run(
        around(lambda at: gm.at[c, at, pl.ds(0, 112)], 1),
        around(lambda at: gm.at[c, at, pl.ds(112, 96)], -1),
        around(lambda at: gt.at[at, pl.ds(c * 16, 16)], 1),
        around(lambda at: qi.at[at, 0, c], 1),
        around(lambda at: qi.at[at, 1, c], -1),
        over_x(),
    )
    own[0].wait()
    own[1].wait()
    for copy in forwards + far:
        copy.wait_recv()
    forwards.clear()
    eye = (
        lax.broadcasted_iota(jnp.int32, (32, 32), 0)
        == lax.broadcasted_iota(jnp.int32, (32, 32), 1)
    ).astype(bf16)
    for b in range(2):
        btt[b] = lax.dot_general(bt[b], eye, TN, preferred_element_type=f32).astype(bf16)

    f_wait()
    f_swap = copies.start(f.at[c, y, xl], f.at[c, y, xl], pair_l)

    def fit_chunk(b):
        def chunk(d):
            part = lax.dot_general(
                bm[0, b], gm[0, d, pl.ds(0, SEQ)], NT, preferred_element_type=f32
            )
            part += lax.dot_general(
                bm[1, b], gm[1, d, pl.ds(0, SEQ)], NT, preferred_element_type=f32
            )
            return part + jnp.dot(btt[b], gt[d], preferred_element_type=f32)[:, :SEQ]

        return chunk

    def query_chunk(d):
        parts = []
        for b in range(2):
            part = lax.dot_general(
                gm[0, d, pl.ds(SEQ, 16)], bm[0, b], NT, preferred_element_type=f32
            )
            part += lax.dot_general(
                gm[1, d, pl.ds(SEQ, 16)], bm[1, b], NT, preferred_element_type=f32
            )
            tail = lax.dot_general(gt[d], bt[b], TN, preferred_element_type=f32)
            parts.append(part + tail[SEQ:TOK])
        return jnp.concatenate(parts, axis=0)

    def fit_done(b):
        def done(total):
            stage[b] = total.astype(bf16)

        return done

    def query_done(total):
        stage_q[0] = total[:16].astype(bf16)
        stage_q[1] = total[16:].astype(bf16)

    run(
        scatter_stream(copies, z, along_z, 1, fit_chunk(0), fit_s.at[0], fit_g.at[0], fit_done(0)),
        scatter_stream(copies, z, along_z, -1, fit_chunk(1), fit_s.at[1], fit_g.at[1], fit_done(1)),
        scatter_stream(copies, z, along_z, 1, query_chunk, qry_s, qry_g, query_done),
        around(lambda at: f.at[c, at, xl], 1),
        around(lambda at: f.at[c, at, 1 - xl], -1, f_swap.wait_recv),
    )
    swap = copies.start(stage.at[1 - xl], landed, pair_l)
    swap_q = copies.start(stage_q.at[1 - xl], landed_q, pair_l)
    rot[xl] = stage[xl]
    qr[z, xh, xl] = stage_q[xl]
    swap_q.wait_recv()
    qr[z, xh, 1 - xl] = landed_q[...]
    q_swap2 = copies.start(qr.at[z, xh], qr.at[z, xh], pair_h)
    swap.wait_recv()
    rot[1 - xl] = landed[...]
    for copy in forwards:
        copy.wait_recv()

    def square_chunk(side):
        def chunk(d):
            first = jnp.dot(rot[0], f[0, d, side], preferred_element_type=f32)
            second = jnp.dot(rot[1], f[1, d, side], preferred_element_type=f32)
            return first * first + second * second

        return chunk

    swaps, sums = [], []

    def far_done(total):
        stage_a[...] = total.astype(bf16)
        swaps.append(copies.start(stage_a, landed_a, pair_h))

    run(
        scatter_stream(
            copies, z, along_z, 1, square_chunk(1 - xh), sq_s.at[0], sq_g.at[0], far_done
        ),
        scatter_stream(
            copies, z, along_z, -1, square_chunk(xh), sq_s.at[1], sq_g.at[1], sums.append
        ),
        gather_stream(copies, z, along_z, 1, lambda at: qr.at[at, xh]),
        gather_stream(
            copies, z, along_z, -1, lambda at: qr.at[at, 1 - xh], None, q_swap2.wait_recv
        ),
    )
    query_sum = lax.dot_general(
        qr[...].reshape(512, PAD), qi[...].reshape(512, 128), TN, preferred_element_type=f32
    )
    swaps[0].wait_recv()
    values = (sums[0] + landed_a[...].astype(f32)) / N_SEQ
    eig[...] = values[:COL]
    s_buf[z, xh] = (query_sum / (values + damping)).astype(bf16)
    s_swap = copies.start(s_buf.at[z, xh], s_buf.at[z, xh], pair_h)

    def across(d, side):
        return pltpu.make_async_remote_copy(
            src_ref=core_s.at[d, side], dst_ref=core_r.at[d, side],
            send_sem=core_send.at[d, side], recv_sem=core_recv.at[d, side],
            device_id=other, device_id_type=pl.DeviceIdType.MESH,
        )

    def to_core(side):
        def ready(d):
            core_s[d, side] = jnp.dot(
                bo[1 - c], s_buf[d, side], preferred_element_type=f32
            ).astype(bf16)
            copy = across(d, side)
            copy.start()
            copies.started.append(copy)

        return ready

    run(
        gather_stream(copies, z, along_z, 1, lambda at: s_buf.at[at, xh], to_core(xh)),
        gather_stream(
            copies, z, along_z, -1, lambda at: s_buf.at[at, 1 - xh], to_core(1 - xh),
            s_swap.wait_recv,
        ),
    )

    def u_chunk(side):
        def chunk(d):
            part = jnp.dot(bo[c], s_buf[d, side], preferred_element_type=f32)
            across(d, side).wait_recv()
            return part + core_r[d, side].astype(f32)

        return chunk

    swaps, sums = [], []

    def u_done(total):
        stage_b[...] = total.astype(bf16)
        swaps.append(copies.start(stage_b, landed_b, pair_l))

    run(
        scatter_stream(copies, y, along_y, 1, u_chunk(1 - xl), u_s.at[0], u_g.at[0], u_done),
        scatter_stream(copies, y, along_y, -1, u_chunk(xl), u_s.at[1], u_g.at[1], sums.append),
    )
    swaps[0].wait_recv()
    u_out[...] = (sums[0] + landed_b[...].astype(f32)).astype(bf16)
    permute(copies, local.at[6], u_out, u_mine, f_to, f_same)()

    def p_chunk(side):
        def chunk(d):
            return lax.dot_general(u_mine[...], bi[2 * d + side], NT, preferred_element_type=f32)

        return chunk

    swaps, sums = [], []

    def p_done(total):
        stage_c[...] = total.astype(bf16)
        swaps.append(copies.start(stage_c, landed_c, pair_h))

    run(
        scatter_stream(copies, z, along_z, 1, p_chunk(1 - xh), p_s.at[0], p_g.at[0], p_done),
        scatter_stream(copies, z, along_z, -1, p_chunk(xh), p_s.at[1], p_g.at[1], sums.append),
    )
    swaps[0].wait_recv()
    pre[...] = (sums[0] + landed_c[...].astype(f32))[:COL].astype(bf16)
    copies.finish()


def per_device(out_grads, layer_inputs, query_grads, query_inputs, basis_out, basis_in):
    shape = jax.ShapeDtypeStruct
    anywhere, vmem = pl.BlockSpec(memory_space=pl.ANY), pl.BlockSpec(memory_space=pltpu.VMEM)
    dma = pltpu.SemaphoreType.DMA

    tokens = jnp.concatenate([out_grads, query_grads], axis=0)
    gm = tokens[:, :MAIN]
    gt = jnp.pad(tokens[:, MAIN:].T, ((0, 12), (0, 48)))
    f = jnp.dot(layer_inputs, basis_in, preferred_element_type=f32).astype(bf16)
    q = jnp.dot(query_inputs, basis_in, preferred_element_type=f32).astype(bf16)
    bm = jnp.pad(basis_out[:MAIN].T, ((0, PAD - COL), (0, 0)))
    bt = jnp.pad(basis_out[MAIN:], ((0, 12), (0, PAD - COL)))
    bo = jnp.pad(
        basis_out.reshape(2, COL, COL), ((0, 0), (0, PAD - COL), (0, PAD - COL))
    )

    def ram(*extent):
        return pltpu.VMEM(extent, bf16)

    def ring(streams, *extent):
        return [ram(*streams, 7, *extent), ram(*streams, 7, *extent)]

    return pl.pallas_call(
        kernel,
        out_shape=[shape((COL, 128), f32), shape((COL, 128), bf16)],
        in_specs=[anywhere] * 6 + [vmem] * 2,
        out_specs=[vmem] * 2,
        scratch_shapes=[
            ram(2, RING, TOK, MAIN),
            ram(RING, 32, 256),
            ram(2, RING, 2, SEQ, 128),
            ram(RING, 2, 2, 16, 128),
            ram(2, 2, PAD, MAIN),
            ram(2, 32, PAD),
            ram(2, PAD, 32),
            *ring((2,), PAD, SEQ),
            *ring((), 32, PAD),
            ram(2, PAD, SEQ),
            ram(PAD, SEQ),
            ram(2, 16, PAD),
            ram(16, PAD),
            ram(2, PAD, SEQ),
            ram(RING, 2, 2, 16, PAD),
            *ring((2,), PAD, 128),
            ram(PAD, 128),
            ram(PAD, 128),
            ram(RING, 2, PAD, 128),
            ram(RING, 2, PAD, 128),
            ram(RING, 2, PAD, 128),
            *ring((2,), PAD, 128),
            ram(PAD, 128),
            ram(PAD, 128),
            ram(PAD, 128),
            ram(PAD, 128),
            *ring((2,), PAD, 128),
            ram(PAD, 128),
            ram(PAD, 128),
            dma((N_SEM,)),
            dma((N_SEM,)),
            dma((RING, 2)),
            dma((RING, 2)),
            dma((7,)),
        ],
        compiler_params=pltpu.CompilerParams(
            collective_id=0, has_side_effects=True, vmem_limit_bytes=56 * 2**20
        ),
    )(gm, gt, f, q, bm, bt, bo, basis_in.reshape(16, 128, 128))


def solution(mesh):
    in_specs = (
        P("dp", "panel"),
        P("dp", None),
        P("dp", "panel"),
        P("dp", None),
        P("panel", "dp"),
        P(None, "panel"),
    )
    out_specs = (P("dp", "panel"), P("dp", "panel"))
    return jax.shard_map(
        per_device, mesh=mesh, in_specs=in_specs, out_specs=out_specs, check_vma=False
    )
```

time: 766 us -> 189 us (0.25)
  waiting for transfers between devices: 557 us -> 0 us
  Pallas kernels: 0 us -> 177 us
  blocking collectives: 131 us -> 0 us
  local copies, waits for them, and re-layouts: 32.9 us -> 9.63 us
  matrix products: 22.7 us -> 1.76 us
  between operations: 14.5 us -> 0.72 us
    psum x2 -> x0, waiting for transfers between devices: 385 us -> none  [the longest x1 233 us: per_device(): lax.psum(part_fit.astype(jnp.bfloat16), 'panel').astype(jnp.float32)]
    pallas_call x0 -> x1, Pallas kernels: none -> 177 us  [per_device(): pl.pallas_call(kernel, out_shape=[shape((COL, 128), f32), shape((COL, 128...]
    all_gather x3 -> x0, waiting for transfers between devices: 166 us -> none  [the longest x1 111 us: per_device(): lax.all_gather(basis_out, 'panel', axis=0, tiled=True)]
    all_gather x2 -> x0, blocking collectives: 66.7 us -> none  [the longest x1 34.3 us: per_device(): lax.all_gather(query_grads, 'dp', axis=0, tiled=True)]
    unnamed x1 -> x0, blocking collectives: 64.4 us -> none
    dot_general x7 -> x2, matrix products: 22.7 us -> 1.76 us  [the longest x1 0.98 us: per_device(): f = jnp.dot(layer_inputs, basis_in, preferred_element_type=f32).astype(bf16)]
    reshape x2, local copies, waits for them, and re-layouts: 14.8 us -> 1.51 us  [per_device(): basis_out.reshape(2, COL, COL)]
    unnamed x15 -> x17, local copies, waits for them, and re-layouts: 12.6 us -> 3.64 us
  transfers between devices with their start and end apart: 7 -> 0, of which waited for: 6 -> 0; matrix products, arithmetic and copies ran while one was open for 6% -> 0% of each run, Pallas kernels for 0% -> 0%
where the time goes in v2:
time: 189 us
  Pallas kernels  177 us (94%)
  local copies, waits for them, and re-layouts  9.63 us (5%)
    pallas_call x1, Pallas kernels, per_device(): pl.pallas_call(kernel, out_shape=[shape((COL, 128), f32), shape((COL, 128...  177 us

profile of v2, /device:TPU:6, one launch (start us, length us, event | category | flops | bytes accessed | tf_op | source)
XLA Modules:
  0.0 189.1 jit_solution(5788162123503002594)
XLA Ops:
  0.6 0.0 copy-start
  0.6 0.0 copy-start.5
  0.7 1.2 copy.13
  1.8 0.0 copy-done.5
  1.8 0.1 copy.14
  2.0 0.1 fusion
  2.1 0.0 copy-start.2
  2.1 0.8 copy.17.gm_in
  2.9 0.1 fusion.1
  3.0 0.6 pad.16.gt_in
  3.6 0.0 copy-done.2
  3.6 0.6 reshape.10
  4.2 0.9 copy.16
  5.1 0.8 pad.19.bo
  5.9 0.0 copy-start.1
  5.9 0.7 pad.17.bm_in
  6.6 0.0 slice-start
  6.6 0.9 slice-done
  7.5 0.1 copy.18
  7.6 0.6 pad.18.bt_in
  8.3 0.0 copy-done
  8.3 0.0 copy-done.1
  8.3 0.0 copy-start.4
  8.3 1.0 convolution_convert_fusion.f_in
  9.3 0.0 copy-done.4
  9.3 0.8 convolution_convert_fusion.1.q_in
  10.0 176.8 %shard_map.77 = (f32[258,128]{1,0:T(8,128)}, bf16[258,128]{1,0:T(8,128)(2,1)}) custom-call(bf16[208,512]{1,0:T(8,128)(2,1)} %copy.17.gm_in, bf16[16,256]{1,0:T(8,128)(2,1)} %pad.16.gt_in, bf16[192,128]{1,0:T(8,128)(2,1)} %convolution_convert_fusion.f_in, bf16[16,128]{1,0:T(8,128)(2,1)} %convolution_convert_fusion.1.q_in, bf16[272,512]{1,0:T(8,128)(2,1)} %pad.17.bm_in, ...), custom_call_target="tpu_custom_call" | custom-call | tf_op jit(solution)/shard_map/pallas_call | solution.py:451
  186.9 0.0 copy-start.3
  186.9 1.6 copy.21
  188.5 0.0 copy-done.3
  188.5 0.6 copy.22
  (1 shorter events, 0.0 us)
Async XLA Ops:
  0.6 7.6 %copy-start = (bf16[192,2048]{1,0:T(8,128)(2,1)S(1)}, bf16[192,2048]{1,0:T(8,128)(2,1)}, u32[]{:S(2)}) copy-start(bf16[192,2048]{1,0:T(8,128)(2,1)} %param.7) | copy-start | bytes 2359300
  0.6 1.2 copy-start.5
  2.1 1.5 copy-start.2
  5.9 2.4 %copy-start.1 = (bf16[2048,128]{1,0:T(8,128)(2,1)S(1)}, bf16[2048,128]{1,0:T(8,128)(2,1)}, u32[]{:S(2)}) copy-start(bf16[2048,128]{1,0:T(8,128)(2,1)} %param.11) | copy-start | bytes 1572868
  6.6 0.9 slice-start
  8.3 1.0 copy-start.4
  186.9 1.6 copy-start.3

commit v3 on v2

--- a/solution.py
+++ b/solution.py
@@ -159,11 +159,18 @@
     done(value + got[3].astype(f32) + got[6].astype(f32))
 
 
+def chosen(rows, columns, shift, limit):
+    r = lax.broadcasted_iota(jnp.int32, (rows, columns), 0)
+    k = lax.broadcasted_iota(jnp.int32, (rows, columns), 1)
+    return jnp.logical_and(k == r + shift, r < limit).astype(f32).astype(bf16)
+
+
 def kernel(
-    gm_in, gt_in, f_in, q_in, bm_in, bt_in, bo, bi, eig, pre,
+    og, li, qg, ql, bout, bin_, eig, pre,
+    gm_in, gt_in, f_in, tt, bo, bia, img,
     gm, gt, f, qi, bm, bt, btt, fit_s, fit_g, qry_s, qry_g, stage, landed, stage_q, landed_q,
     rot, qr, sq_s, sq_g, stage_a, landed_a, s_buf, core_s, core_r, u_s, u_g, stage_b, landed_b,
-    u_out, u_mine, p_s, p_g, stage_c, landed_c, send, recv, core_send, core_recv, local,
+    u_out, u_mine, send, recv, core_send, core_recv, local,
 ):
     y, xl, c, z, xh = coords()
     x = xh * 2 + xl
@@ -188,12 +195,30 @@
     def _():
         signal(f_to)
 
+    gm_in[pl.ds(0, SEQ)] = og[:, :MAIN]
+    gm_in[pl.ds(SEQ, 16)] = qg[:, :MAIN]
+    tt[...] = jnp.zeros_like(tt)
+    tt[pl.ds(0, SEQ), pl.ds(0, 4)] = og[:, MAIN:]
+    tt[pl.ds(SEQ, 16), pl.ds(0, 4)] = qg[:, MAIN:]
+    gt_in[...] = lax.dot_general(
+        chosen(16, 128, 0, 4), tt[...], NT, preferred_element_type=f32
+    ).astype(bf16)
+
     wait_all(10 - g_same.astype(jnp.int32) - f_same.astype(jnp.int32))
     copies = Copies(send, recv)
 
     g_wait = permute(copies, local.at[0], gm_in, gm.at[xh, y], g_to, g_same)
     t_wait = permute(copies, local.at[1], gt_in, gt.at[y, pl.ds(xh * 16, 16)], g_to, g_same)
-    f_wait = permute(copies, local.at[2], f_in, f.at[c, z, xh], f_to, f_same)
+
+    quarter = xl * 2 + c
+
+    def bi_at(group, block):
+        return bia.at[group, :, pl.ds(pl.multiple_of(block * 128, 128), 128)]
+
+    own_bi = pltpu.make_async_copy(
+        bin_.at[pl.ds(quarter * 512, 512)], bi_at(quarter, xh * 8 + z), local.at[3]
+    )
+    own_bi.start()
 
     def bm_at(q):
         return bm.at[lax.div(q, 2), lax.rem(q, 2)]
@@ -201,18 +226,20 @@
     def bt_at(q):
         return bt.at[lax.rem(q, 2), pl.ds(lax.div(q, 2) * 16, 16)]
 
-    own = [
-        pltpu.make_async_copy(bm_in, bm_at(x), local.at[3]),
-        pltpu.make_async_copy(bt_in, bt_at(x), local.at[4]),
-        pltpu.make_async_copy(q_in, qi.at[y, xl, c], local.at[5]),
-    ]
-    for copy in own:
-        copy.start()
-    m_right = copies.start(bm_in, bm_at(x), right)
-    m_left = copies.start(bm_in, bm_at(x), left)
-    t_right = copies.start(bt_in, bt_at(x), right)
-    t_left = copies.start(bt_in, bt_at(x), left)
-    q_swap = copies.start(q_in, qi.at[y, xl, c], pair_l)
+    bm[xh, xl] = lax.dot_general(
+        chosen(PAD, COL, 0, COL), bout[pl.ds(0, MAIN)], NT, preferred_element_type=f32
+    ).astype(bf16)
+    m_right = copies.start(bm_at(x), bm_at(x), right)
+    m_left = copies.start(bm_at(x), bm_at(x), left)
+    bt_own = bt_at(x)
+    bt_own[...] = jnp.zeros((16, PAD), bf16)
+    bt_own[pl.ds(0, 4), pl.ds(0, COL)] = bout[pl.ds(MAIN, 4)]
+    t_right = copies.start(bt_own, bt_own, right)
+    t_left = copies.start(bt_own, bt_own, left)
+    qi[y, xl, c] = jnp.dot(ql[...], bin_[...], preferred_element_type=f32).astype(bf16)
+    q_swap = copies.start(qi.at[y, xl, c], qi.at[y, xl, c], pair_l)
+    f_in[...] = jnp.dot(li[...], bin_[...], preferred_element_type=f32).astype(bf16)
+    f_wait = permute(copies, local.at[2], f_in, f.at[c, z, xh], f_to, f_same)
 
     forwards = []
 
@@ -225,7 +252,7 @@
     def around(slot, sign, first=None):
         return gather_stream(copies, y, along_y, sign, slot, pass_on(slot), first)
 
-    own[2].wait()
+    own_bi.wait()
     q_swap.wait_recv()
     g_wait()
     t_wait()
@@ -252,9 +279,28 @@
         around(lambda at: qi.at[at, 0, c], 1),
         around(lambda at: qi.at[at, 1, c], -1),
         over_x(),
-    )
-    own[0].wait()
-    own[1].wait()
+        gather_stream(
+            copies, z, along_z, 1, lambda at: bi_at(quarter, xh * 8 + at).at[pl.ds(0, 256)]
+        ),
+        gather_stream(
+            copies, z, along_z, -1, lambda at: bi_at(quarter, xh * 8 + at).at[pl.ds(256, 256)]
+        ),
+    )
+
+    def quarter_at(q, low=0, count=512):
+        lanes = pl.ds(pl.multiple_of(lax.div(q, 2) * 1024, 1024), 1024)
+        return bia.at[lax.rem(q, 2) * 2 + c, pl.ds(low, count), lanes]
+
+    x_l, x_r, x_f = lax.rem(x + 3, 4), lax.rem(x + 1, 4), lax.rem(x + 2, 4)
+    i_right = copies.start(quarter_at(x), quarter_at(x), right)
+    i_left = copies.start(quarter_at(x), quarter_at(x), left)
+    i_core = [copies.start(quarter_at(x), quarter_at(x), other)]
+
+    for h in range(2):
+        bo[h] = jnp.zeros((PAD, PAD), bf16)
+        bo[h, :, pl.ds(0, COL)] = jnp.dot(
+            chosen(PAD, 2 * COL, h * COL, COL), bout[...], preferred_element_type=f32
+        ).astype(bf16)
     for copy in forwards + far:
         copy.wait_recv()
     forwards.clear()
@@ -321,6 +367,12 @@
     rot[1 - xl] = landed[...]
     for copy in forwards:
         copy.wait_recv()
+    i_right.wait_recv()
+    i_far = [copies.start(quarter_at(x_l, 0, 256), quarter_at(x_l, 0, 256), right)]
+    i_left.wait_recv()
+    i_far.append(copies.start(quarter_at(x_r, 256, 256), quarter_at(x_r, 256, 256), left))
+    for q in (x_l, x_r):
+        i_core.append(copies.start(quarter_at(q), quarter_at(q), other))
 
     def square_chunk(side):
         def chunk(d):
@@ -351,11 +403,35 @@
     query_sum = lax.dot_general(
         qr[...].reshape(512, PAD), qi[...].reshape(512, 128), TN, preferred_element_type=f32
     )
+    for copy in i_far:
+        copy.wait_recv()
+    i_core.append(copies.start(quarter_at(x_f), quarter_at(x_f), other))
     swaps[0].wait_recv()
     values = (sums[0] + landed_a[...].astype(f32)) / N_SEQ
     eig[...] = values[:COL]
-    s_buf[z, xh] = (query_sum / (values + damping)).astype(bf16)
-    s_swap = copies.start(s_buf.at[z, xh], s_buf.at[z, xh], pair_h)
+
+    def s_at(side, at):
+        return s_buf.at[:, pl.ds(pl.multiple_of((side * 8 + at) * 128, 128), 128)]
+
+    s_own = s_at(xh, z)
+    s_own[...] = (query_sum / (values + damping)).astype(bf16)
+    s_swap = copies.start(s_own, s_own, pair_h)
+    run(
+        gather_stream(copies, z, along_z, 1, lambda at: s_at(xh, at)),
+        gather_stream(
+            copies, z, along_z, -1, lambda at: s_at(1 - xh, at), None, s_swap.wait_recv
+        ),
+    )
+    for copy in i_core:
+        copy.wait_recv()
+
+    def image(group, carry):
+        value = lax.dot_general(s_buf[...], bia[group], NT, preferred_element_type=f32)
+        for j in range(4):
+            img[group * 4 + j] = value[:, j * 128 : (j + 1) * 128].astype(bf16)
+        return carry
+
+    lax.fori_loop(0, 4, image, 0)
 
     def across(d, side):
         return pltpu.make_async_remote_copy(
@@ -364,28 +440,19 @@
             device_id=other, device_id_type=pl.DeviceIdType.MESH,
         )
 
-    def to_core(side):
-        def ready(d):
+    for by in (4, -3, 3, -2, 2, -1, 1, 0):
+        d = turn(y, by)
+        for side in range(2):
             core_s[d, side] = jnp.dot(
-                bo[1 - c], s_buf[d, side], preferred_element_type=f32
+                bo[1 - c], img[2 * d + side], preferred_element_type=f32
             ).astype(bf16)
             copy = across(d, side)
             copy.start()
             copies.started.append(copy)
 
-        return ready
-
-    run(
-        gather_stream(copies, z, along_z, 1, lambda at: s_buf.at[at, xh], to_core(xh)),
-        gather_stream(
-            copies, z, along_z, -1, lambda at: s_buf.at[at, 1 - xh], to_core(1 - xh),
-            s_swap.wait_recv,
-        ),
-    )
-
     def u_chunk(side):
         def chunk(d):
-            part = jnp.dot(bo[c], s_buf[d, side], preferred_element_type=f32)
+            part = jnp.dot(bo[c], img[2 * d + side], preferred_element_type=f32)
             across(d, side).wait_recv()
             return part + core_r[d, side].astype(f32)
 
@@ -403,44 +470,15 @@
     )
     swaps[0].wait_recv()
     u_out[...] = (sums[0] + landed_b[...].astype(f32)).astype(bf16)
-    permute(copies, local.at[6], u_out, u_mine, f_to, f_same)()
-
-    def p_chunk(side):
-        def chunk(d):
-            return lax.dot_general(u_mine[...], bi[2 * d + side], NT, preferred_element_type=f32)
-
-        return chunk
-
-    swaps, sums = [], []
-
-    def p_done(total):
-        stage_c[...] = total.astype(bf16)
-        swaps.append(copies.start(stage_c, landed_c, pair_h))
-
-    run(
-        scatter_stream(copies, z, along_z, 1, p_chunk(1 - xh), p_s.at[0], p_g.at[0], p_done),
-        scatter_stream(copies, z, along_z, -1, p_chunk(xh), p_s.at[1], p_g.at[1], sums.append),
-    )
-    swaps[0].wait_recv()
-    pre[...] = (sums[0] + landed_c[...].astype(f32))[:COL].astype(bf16)
+    permute(copies, local.at[4], u_out, u_mine, f_to, f_same)()
+    pre[...] = u_mine[pl.ds(0, COL)]
     copies.finish()
 
 
 def per_device(out_grads, layer_inputs, query_grads, query_inputs, basis_out, basis_in):
     shape = jax.ShapeDtypeStruct
-    anywhere, vmem = pl.BlockSpec(memory_space=pl.ANY), pl.BlockSpec(memory_space=pltpu.VMEM)
+    vmem = pl.BlockSpec(memory_space=pltpu.VMEM)
     dma = pltpu.SemaphoreType.DMA
-
-    tokens = jnp.concatenate([out_grads, query_grads], axis=0)
-    gm = tokens[:, :MAIN]
-    gt = jnp.pad(tokens[:, MAIN:].T, ((0, 12), (0, 48)))
-    f = jnp.dot(layer_inputs, basis_in, preferred_element_type=f32).astype(bf16)
-    q = jnp.dot(query_inputs, basis_in, preferred_element_type=f32).astype(bf16)
-    bm = jnp.pad(basis_out[:MAIN].T, ((0, PAD - COL), (0, 0)))
-    bt = jnp.pad(basis_out[MAIN:], ((0, 12), (0, PAD - COL)))
-    bo = jnp.pad(
-        basis_out.reshape(2, COL, COL), ((0, 0), (0, PAD - COL), (0, PAD - COL))
-    )
 
     def ram(*extent):
         return pltpu.VMEM(extent, bf16)
@@ -451,9 +489,16 @@
     return pl.pallas_call(
         kernel,
         out_shape=[shape((COL, 128), f32), shape((COL, 128), bf16)],
-        in_specs=[anywhere] * 6 + [vmem] * 2,
+        in_specs=[vmem] * 6,
         out_specs=[vmem] * 2,
         scratch_shapes=[
+            ram(TOK, MAIN),
+            ram(16, 256),
+            ram(SEQ, 128),
+            ram(256, 128),
+            ram(2, PAD, PAD),
+            ram(4, 512, 2048),
+            ram(16, PAD, 128),
             ram(2, RING, TOK, MAIN),
             ram(RING, 32, 256),
             ram(2, RING, 2, SEQ, 128),
@@ -472,7 +517,7 @@
             *ring((2,), PAD, 128),
             ram(PAD, 128),
             ram(PAD, 128),
-            ram(RING, 2, PAD, 128),
+            ram(PAD, 2048),
             ram(RING, 2, PAD, 128),
             ram(RING, 2, PAD, 128),
             *ring((2,), PAD, 128),
@@ -480,19 +525,16 @@
             ram(PAD, 128),
             ram(PAD, 128),
             ram(PAD, 128),
-            *ring((2,), PAD, 128),
-            ram(PAD, 128),
-            ram(PAD, 128),
             dma((N_SEM,)),
             dma((N_SEM,)),
             dma((RING, 2)),
             dma((RING, 2)),
-            dma((7,)),
+            dma((5,)),
         ],
         compiler_params=pltpu.CompilerParams(
             collective_id=0, has_side_effects=True, vmem_limit_bytes=56 * 2**20
         ),
-    )(gm, gt, f, q, bm, bt, bo, basis_in.reshape(16, 128, 128))
+    )(out_grads, layer_inputs, query_grads, query_inputs, basis_out, basis_in)
 
 
 def solution(mesh):

time: 189 us -> 180 us (0.952)
  the two profiles are of different devices: /device:TPU:6 before, /device:TPU:60 now
where the time goes in v3:
time: 180 us
  Pallas kernels  175 us (97%)
  local copies, waits for them, and re-layouts  4.15 us (2%)
    pallas_call x1, Pallas kernels, per_device(): pl.pallas_call(kernel, out_shape=[shape((COL, 128), f32), shape((COL, 128...  175 us
    unnamed x5, local copies, waits for them, and re-layouts  4.15 us

profile of v3, /device:TPU:60, one launch (start us, length us, event | category | flops | bytes accessed | tf_op | source)
XLA Modules:
  0.0 179.8 jit_solution(15374940156974375302)
XLA Ops:
  0.6 1.9 %copy.8.bout = bf16[516,258]{1,0:T(8,128)(2,1)} copy(bf16[516,258]{0,1:T(8,128)(2,1)} %param.10) | data formatting | bytes 532512 | tf_op args[4]
  2.5 175.0 %shard_map.77 = (f32[258,128]{1,0:T(8,128)}, bf16[258,128]{1,0:T(8,128)(2,1)}) custom-call(bf16[192,516]{1,0:T(8,128)(2,1)} %og.1, bf16[192,2048]{1,0:T(8,128)(2,1)} %li.1, bf16[16,516]{1,0:T(8,128)(2,1)} %qg.1, bf16[16,2048]{1,0:T(8,128)(2,1)} %ql.1, bf16[516,258]{1,0:T(8,128)(2,1)} %copy.8.bout, bf16[2048,128]{1,0:T(8,128)(2,1)} %bin_.1), custom_call_target="tpu_custom_call" | custom-call | tf_op jit(solution)/shard_map/pallas_call | solution.py:489
  177.6 0.0 copy-start
  177.6 1.6 copy.11
  179.2 0.0 copy-done
  179.2 0.6 copy.12
Async XLA Ops:
  177.6 1.6 copy-start

commit v4 on v3

--- a/solution.py
+++ b/solution.py
@@ -15,9 +15,10 @@
 MAIN = 512
 N_SEQ = 32
 RING = 8
+PARTS = ((0, 144), (144, 128))
 NT = (((1,), (1,)), ((), ()))
 TN = (((0,), (0,)), ((), ()))
-N_SEM = 256
+N_SEM = 320
 
 
 def coords():
@@ -137,7 +138,7 @@
     ahead, back = ways[::sign]
     a = b = None
     for t in range(4):
-        value = chunk(turn(pos, sign * (4 - t)))
+        value = chunk(turn(pos, 4 - t) if sign > 0 else turn(pos, t - 4), 4 - t)
         if t:
             yield
             a.wait_recv()
@@ -145,14 +146,14 @@
         sent[t] = value.astype(bf16)
         a = copies.start(sent.at[t], got.at[t], ahead)
         if t < 3:
-            value = chunk(turn(pos, sign * (t - 3)))
+            value = chunk(turn(pos, t - 3) if sign > 0 else turn(pos, 3 - t), t - 3)
             if t:
                 yield
                 b.wait_recv()
                 value = value + got[3 + t].astype(f32)
             sent[4 + t] = value.astype(bf16)
             b = copies.start(sent.at[4 + t], got.at[4 + t], back)
-    value = chunk(pos)
+    value = chunk(pos, 0)
     yield
     a.wait_recv()
     b.wait_recv()
@@ -168,8 +169,7 @@
 def kernel(
     og, li, qg, ql, bout, bin_, eig, pre,
     gm_in, gt_in, f_in, tt, bo, bia, img,
-    gm, gt, f, qi, bm, bt, btt, fit_s, fit_g, qry_s, qry_g, stage, landed, stage_q, landed_q,
-    rot, qr, sq_s, sq_g, stage_a, landed_a, s_buf, core_s, core_r, u_s, u_g, stage_b, landed_b,
+    gm, gt, f, qi, bm, bt, btt, fit_s, fit_g, stage, landed, rot, qr, sq_s, sq_g, stage_a, landed_a, s_buf, core_s, core_r, u_s, u_g, stage_b, landed_b,
     u_out, u_mine, send, recv, core_send, core_recv, local,
 ):
     y, xl, c, z, xh = coords()
@@ -229,13 +229,9 @@
     bm[xh, xl] = lax.dot_general(
         chosen(PAD, COL, 0, COL), bout[pl.ds(0, MAIN)], NT, preferred_element_type=f32
     ).astype(bf16)
-    m_right = copies.start(bm_at(x), bm_at(x), right)
-    m_left = copies.start(bm_at(x), bm_at(x), left)
     bt_own = bt_at(x)
     bt_own[...] = jnp.zeros((16, PAD), bf16)
     bt_own[pl.ds(0, 4), pl.ds(0, COL)] = bout[pl.ds(MAIN, 4)]
-    t_right = copies.start(bt_own, bt_own, right)
-    t_left = copies.start(bt_own, bt_own, left)
     qi[y, xl, c] = jnp.dot(ql[...], bin_[...], preferred_element_type=f32).astype(bf16)
     q_swap = copies.start(qi.at[y, xl, c], qi.at[y, xl, c], pair_l)
     f_in[...] = jnp.dot(li[...], bin_[...], preferred_element_type=f32).astype(bf16)
@@ -256,6 +252,10 @@
     q_swap.wait_recv()
     g_wait()
     t_wait()
+    m_right = copies.start(bm_at(x), bm_at(x), right)
+    m_left = copies.start(bm_at(x), bm_at(x), left)
+    t_right = copies.start(bt_own, bt_own, right)
+    t_left = copies.start(bt_own, bt_own, left)
     far = []
 
     def over_x():
@@ -314,114 +314,125 @@
     f_wait()
     f_swap = copies.start(f.at[c, y, xl], f.at[c, y, xl], pair_l)
 
-    def fit_chunk(b):
-        def chunk(d):
-            part = lax.dot_general(
-                bm[0, b], gm[0, d, pl.ds(0, SEQ)], NT, preferred_element_type=f32
+    def fit_stream(b, part):
+        low, count = PARTS[part]
+
+        def chunk(d, by):
+            value = lax.dot_general(
+                bm[0, b, pl.ds(low, count)], gm[0, d], NT, preferred_element_type=f32
             )
-            part += lax.dot_general(
-                bm[1, b], gm[1, d, pl.ds(0, SEQ)], NT, preferred_element_type=f32
+            value += lax.dot_general(
+                bm[1, b, pl.ds(low, count)], gm[1, d], NT, preferred_element_type=f32
             )
-            return part + jnp.dot(btt[b], gt[d], preferred_element_type=f32)[:, :SEQ]
-
-        return chunk
-
-    def query_chunk(d):
-        parts = []
-        for b in range(2):
-            part = lax.dot_general(
-                gm[0, d, pl.ds(SEQ, 16)], bm[0, b], NT, preferred_element_type=f32
-            )
-            part += lax.dot_general(
-                gm[1, d, pl.ds(SEQ, 16)], bm[1, b], NT, preferred_element_type=f32
-            )
-            tail = lax.dot_general(gt[d], bt[b], TN, preferred_element_type=f32)
-            parts.append(part + tail[SEQ:TOK])
-        return jnp.concatenate(parts, axis=0)
-
-    def fit_done(b):
+            tail = jnp.dot(btt[b, pl.ds(low, count)], gt[d], preferred_element_type=f32)
+            return value + tail[:, :TOK]
+
         def done(total):
-            stage[b] = total.astype(bf16)
-
-        return done
-
-    def query_done(total):
-        stage_q[0] = total[:16].astype(bf16)
-        stage_q[1] = total[16:].astype(bf16)
+            stage[b, pl.ds(low, count)] = total.astype(bf16)
+
+        return scatter_stream(
+            copies, z, along_z, 1 - 2 * b, chunk,
+            fit_s.at[b, :, pl.ds(low, count)], fit_g.at[b, :, pl.ds(low, count)], done,
+        )
 
     run(
-        scatter_stream(copies, z, along_z, 1, fit_chunk(0), fit_s.at[0], fit_g.at[0], fit_done(0)),
-        scatter_stream(copies, z, along_z, -1, fit_chunk(1), fit_s.at[1], fit_g.at[1], fit_done(1)),
-        scatter_stream(copies, z, along_z, 1, query_chunk, qry_s, qry_g, query_done),
+        fit_stream(0, 0), fit_stream(1, 0), fit_stream(0, 1), fit_stream(1, 1),
         around(lambda at: f.at[c, at, xl], 1),
         around(lambda at: f.at[c, at, 1 - xl], -1, f_swap.wait_recv),
     )
     swap = copies.start(stage.at[1 - xl], landed, pair_l)
-    swap_q = copies.start(stage_q.at[1 - xl], landed_q, pair_l)
     rot[xl] = stage[xl]
-    qr[z, xh, xl] = stage_q[xl]
-    swap_q.wait_recv()
-    qr[z, xh, 1 - xl] = landed_q[...]
-    q_swap2 = copies.start(qr.at[z, xh], qr.at[z, xh], pair_h)
     swap.wait_recv()
     rot[1 - xl] = landed[...]
+    for h in range(2):
+        qr[z, xh, h] = lax.dot_general(
+            chosen(16, TOK, SEQ, 16), rot[h], NT, preferred_element_type=f32
+        ).astype(bf16)
+    q_swap2 = copies.start(qr.at[z, xh], qr.at[z, xh], pair_h)
     for copy in forwards:
         copy.wait_recv()
-    i_right.wait_recv()
-    i_far = [copies.start(quarter_at(x_l, 0, 256), quarter_at(x_l, 0, 256), right)]
-    i_left.wait_recv()
-    i_far.append(copies.start(quarter_at(x_r, 256, 256), quarter_at(x_r, 256, 256), left))
-    for q in (x_l, x_r):
-        i_core.append(copies.start(quarter_at(q), quarter_at(q), other))
-
-    def square_chunk(side):
-        def chunk(d):
-            first = jnp.dot(rot[0], f[0, d, side], preferred_element_type=f32)
-            second = jnp.dot(rot[1], f[1, d, side], preferred_element_type=f32)
+    i_far = []
+
+    def bi_over_x():
+        for _ in range(3):
+            yield
+        i_right.wait_recv()
+        i_far.append(copies.start(quarter_at(x_l, 0, 256), quarter_at(x_l, 0, 256), right))
+        i_left.wait_recv()
+        i_far.append(copies.start(quarter_at(x_r, 256, 256), quarter_at(x_r, 256, 256), left))
+        for q in (x_l, x_r):
+            i_core.append(copies.start(quarter_at(q), quarter_at(q), other))
+
+    def bi_far():
+        for _ in range(3):
+            yield
+        for copy in i_far:
+            copy.wait_recv()
+        i_core.append(copies.start(quarter_at(x_f), quarter_at(x_f), other))
+
+    swaps, sums = {}, {}
+
+    def square_stream(near, part):
+        low, count = PARTS[part]
+        side = xh if near else 1 - xh
+
+        def chunk(d, by):
+            first = jnp.dot(
+                rot[0, pl.ds(low, count), pl.ds(0, SEQ)], f[0, d, side],
+                preferred_element_type=f32,
+            )
+            second = jnp.dot(
+                rot[1, pl.ds(low, count), pl.ds(0, SEQ)], f[1, d, side],
+                preferred_element_type=f32,
+            )
             return first * first + second * second
 
-        return chunk
-
-    swaps, sums = [], []
-
-    def far_done(total):
-        stage_a[...] = total.astype(bf16)
-        swaps.append(copies.start(stage_a, landed_a, pair_h))
+        def done(total):
+            if near:
+                sums[part] = total
+            else:
+                half = stage_a.at[pl.ds(low, count)]
+                half[...] = total.astype(bf16)
+                swaps[part] = copies.start(half, landed_a.at[pl.ds(low, count)], pair_h)
+
+        return scatter_stream(
+            copies, z, along_z, -1 if near else 1, chunk,
+            sq_s.at[near, :, pl.ds(low, count)], sq_g.at[near, :, pl.ds(low, count)], done,
+        )
 
     run(
-        scatter_stream(
-            copies, z, along_z, 1, square_chunk(1 - xh), sq_s.at[0], sq_g.at[0], far_done
-        ),
-        scatter_stream(
-            copies, z, along_z, -1, square_chunk(xh), sq_s.at[1], sq_g.at[1], sums.append
-        ),
+        square_stream(0, 0), square_stream(1, 0), square_stream(0, 1), square_stream(1, 1),
         gather_stream(copies, z, along_z, 1, lambda at: qr.at[at, xh]),
         gather_stream(
             copies, z, along_z, -1, lambda at: qr.at[at, 1 - xh], None, q_swap2.wait_recv
         ),
+        bi_over_x(),
     )
     query_sum = lax.dot_general(
         qr[...].reshape(512, PAD), qi[...].reshape(512, 128), TN, preferred_element_type=f32
     )
-    for copy in i_far:
-        copy.wait_recv()
-    i_core.append(copies.start(quarter_at(x_f), quarter_at(x_f), other))
-    swaps[0].wait_recv()
-    values = (sums[0] + landed_a[...].astype(f32)) / N_SEQ
-    eig[...] = values[:COL]
-
-    def s_at(side, at):
-        return s_buf.at[:, pl.ds(pl.multiple_of((side * 8 + at) * 128, 128), 128)]
-
-    s_own = s_at(xh, z)
-    s_own[...] = (query_sum / (values + damping)).astype(bf16)
-    s_swap = copies.start(s_own, s_own, pair_h)
-    run(
-        gather_stream(copies, z, along_z, 1, lambda at: s_at(xh, at)),
-        gather_stream(
-            copies, z, along_z, -1, lambda at: s_at(1 - xh, at), None, s_swap.wait_recv
-        ),
-    )
+    def s_at(side, at, part):
+        low, count = PARTS[part]
+        lanes = pl.ds(pl.multiple_of((side * 8 + at) * 128, 128), 128)
+        return s_buf.at[pl.ds(low, count), lanes]
+
+    def s_streams(part):
+        low, count = PARTS[part]
+        swaps[part].wait_recv()
+        values = (sums[part] + landed_a[pl.ds(low, count)].astype(f32)) / N_SEQ
+        kept = min(count, COL - low)
+        eig[pl.ds(low, kept)] = values[:kept]
+        own = s_at(xh, z, part)
+        own[...] = (query_sum[low : low + count] / (values + damping)).astype(bf16)
+        swap = copies.start(own, own, pair_h)
+        return (
+            gather_stream(copies, z, along_z, 1, lambda at: s_at(xh, at, part)),
+            gather_stream(
+                copies, z, along_z, -1, lambda at: s_at(1 - xh, at, part), None, swap.wait_recv
+            ),
+        )
+
+    run(*s_streams(0), *s_streams(1), bi_far())
     for copy in i_core:
         copy.wait_recv()
 
@@ -450,27 +461,47 @@
             copy.start()
             copies.started.append(copy)
 
-    def u_chunk(side):
-        def chunk(d):
-            part = jnp.dot(bo[c], img[2 * d + side], preferred_element_type=f32)
-            across(d, side).wait_recv()
-            return part + core_r[d, side].astype(f32)
-
-        return chunk
-
-    swaps, sums = [], []
-
-    def u_done(total):
-        stage_b[...] = total.astype(bf16)
-        swaps.append(copies.start(stage_b, landed_b, pair_l))
-
-    run(
-        scatter_stream(copies, y, along_y, 1, u_chunk(1 - xl), u_s.at[0], u_g.at[0], u_done),
-        scatter_stream(copies, y, along_y, -1, u_chunk(xl), u_s.at[1], u_g.at[1], sums.append),
-    )
-    swaps[0].wait_recv()
-    u_out[...] = (sums[0] + landed_b[...].astype(f32)).astype(bf16)
-    permute(copies, local.at[4], u_out, u_mine, f_to, f_same)()
+    swaps, sums, seen = {}, {}, set()
+
+    def u_stream(near, part):
+        low, count = PARTS[part]
+        side = xl if near else 1 - xl
+
+        def chunk(d, by):
+            value = jnp.dot(
+                bo[c, pl.ds(low, count)], img[2 * d + side], preferred_element_type=f32
+            )
+            if (near, by) not in seen:
+                seen.add((near, by))
+                across(d, side).wait_recv()
+            return value + core_r[d, side, pl.ds(low, count)].astype(f32)
+
+        def done(total):
+            if near:
+                sums[part] = total
+            else:
+                half = stage_b.at[pl.ds(low, count)]
+                half[...] = total.astype(bf16)
+                swaps[part] = copies.start(half, landed_b.at[pl.ds(low, count)], pair_l)
+
+        return scatter_stream(
+            copies, y, along_y, -1 if near else 1, chunk,
+            u_s.at[near, :, pl.ds(low, count)], u_g.at[near, :, pl.ds(low, count)], done,
+        )
+
+    run(u_stream(0, 0), u_stream(1, 0), u_stream(0, 1), u_stream(1, 1))
+    waits = []
+    for part, (low, count) in enumerate(PARTS):
+        swaps[part].wait_recv()
+        half = u_out.at[pl.ds(low, count)]
+        half[...] = (sums[part] + landed_b[pl.ds(low, count)].astype(f32)).astype(bf16)
+        waits.append(
+            permute(
+                copies, local.at[4 + part], half, u_mine.at[pl.ds(low, count)], f_to, f_same
+            )
+        )
+    for wait in waits:
+        wait()
     pre[...] = u_mine[pl.ds(0, COL)]
     copies.finish()
 
@@ -506,13 +537,10 @@
             ram(2, 2, PAD, MAIN),
             ram(2, 32, PAD),
             ram(2, PAD, 32),
-            *ring((2,), PAD, SEQ),
-            *ring((), 32, PAD),
-            ram(2, PAD, SEQ),
-            ram(PAD, SEQ),
-            ram(2, 16, PAD),
-            ram(16, PAD),
-            ram(2, PAD, SEQ),
+            *ring((2,), PAD, TOK),
+            ram(2, PAD, TOK),
+            ram(PAD, TOK),
+            ram(2, PAD, TOK),
             ram(RING, 2, 2, 16, PAD),
             *ring((2,), PAD, 128),
             ram(PAD, 128),
@@ -529,7 +557,7 @@
             dma((N_SEM,)),
             dma((RING, 2)),
             dma((RING, 2)),
-            dma((5,)),
+            dma((6,)),
         ],
         compiler_params=pltpu.CompilerParams(
             collective_id=0, has_side_effects=True, vmem_limit_bytes=56 * 2**20

time: 180 us -> 172 us (0.956)
  the two profiles are of different devices: /device:TPU:60 before, /device:TPU:2 now
where the time goes in v4:
time: 172 us; the launch traced here: 171 us
  Pallas kernels  167 us (97%)
  local copies, waits for them, and re-layouts  4.15 us (2%)
    pallas_call x1, Pallas kernels, per_device(): pl.pallas_call(kernel, out_shape=[shape((COL, 128), f32), shape((COL, 128...  167 us
    unnamed x5, local copies, waits for them, and re-layouts  4.15 us

profile of v4, /device:TPU:2, one launch (start us, length us, event | category | flops | bytes accessed | tf_op | source)
XLA Modules:
  0.0 171.4 jit_solution(2159183554590522664)
XLA Ops:
  0.6 1.9 %copy.8.bout = bf16[516,258]{1,0:T(8,128)(2,1)} copy(bf16[516,258]{0,1:T(8,128)(2,1)} %param.10) | data formatting | bytes 532512 | tf_op args[4]
  2.5 166.6 %shard_map.77 = (f32[258,128]{1,0:T(8,128)}, bf16[258,128]{1,0:T(8,128)(2,1)}) custom-call(bf16[192,516]{1,0:T(8,128)(2,1)} %og.1, bf16[192,2048]{1,0:T(8,128)(2,1)} %li.1, bf16[16,516]{1,0:T(8,128)(2,1)} %qg.1, bf16[16,2048]{1,0:T(8,128)(2,1)} %ql.1, bf16[516,258]{1,0:T(8,128)(2,1)} %copy.8.bout, bf16[2048,128]{1,0:T(8,128)(2,1)} %bin_.1), custom_call_target="tpu_custom_call" | custom-call | tf_op jit(solution)/shard_map/pallas_call | solution.py:520
  169.1 0.0 copy-start
  169.1 1.6 copy.11
  170.8 0.0 copy-done
  170.8 0.6 copy.12
Async XLA Ops:
  169.1 1.6 copy-start

commit v5 on v4

--- a/solution.py
+++ b/solution.py
@@ -105,6 +105,19 @@
                 next(stream)
             except StopIteration:
                 live.remove(stream)
+
+
+class Ahead:
+    def __init__(self, make, lead):
+        self.make, self.lead, self.made = make, lead, 0
+
+    def need(self, off):
+        order = (4, 5, 3, 6, 2, 7, 1, 0)
+        last = min(order.index(off % RING) + 1 + self.lead, RING)
+        while self.made < last:
+            self.make(order[self.made])
+            self.made += 1
+        return off % RING
 
 
 def gather_stream(copies, pos, ways, sign, slot, ready=None, first=None):
@@ -134,11 +147,11 @@
                 ready(at)
 
 
-def scatter_stream(copies, pos, ways, sign, chunk, sent, got, done):
+def scatter_stream(copies, ways, sign, chunk, sent, got, done):
     ahead, back = ways[::sign]
     a = b = None
     for t in range(4):
-        value = chunk(turn(pos, 4 - t) if sign > 0 else turn(pos, t - 4), 4 - t)
+        value = chunk(sign * (4 - t))
         if t:
             yield
             a.wait_recv()
@@ -146,14 +159,14 @@
         sent[t] = value.astype(bf16)
         a = copies.start(sent.at[t], got.at[t], ahead)
         if t < 3:
-            value = chunk(turn(pos, t - 3) if sign > 0 else turn(pos, 3 - t), t - 3)
+            value = chunk(sign * (t - 3))
             if t:
                 yield
                 b.wait_recv()
                 value = value + got[3 + t].astype(f32)
             sent[4 + t] = value.astype(bf16)
             b = copies.start(sent.at[4 + t], got.at[4 + t], back)
-    value = chunk(pos, 0)
+    value = chunk(0)
     yield
     a.wait_recv()
     b.wait_recv()
@@ -171,6 +184,7 @@
     gm_in, gt_in, f_in, tt, bo, bia, img,
     gm, gt, f, qi, bm, bt, btt, fit_s, fit_g, stage, landed, rot, qr, sq_s, sq_g, stage_a, landed_a, s_buf, core_s, core_r, u_s, u_g, stage_b, landed_b,
     u_out, u_mine, send, recv, core_send, core_recv, local,
+    fit_v, pair_v,
 ):
     y, xl, c, z, xh = coords()
     x = xh * 2 + xl
@@ -212,13 +226,20 @@
 
     quarter = xl * 2 + c
 
-    def bi_at(group, block):
-        return bia.at[group, :, pl.ds(pl.multiple_of(block * 128, 128), 128)]
-
-    own_bi = pltpu.make_async_copy(
-        bin_.at[pl.ds(quarter * 512, 512)], bi_at(quarter, xh * 8 + z), local.at[3]
-    )
-    own_bi.start()
+    def bi_at(block, low=0, count=128):
+        return bia.at[quarter, pl.ds(pl.multiple_of(block * 128 + low, 64), count)]
+
+    bi_own = bi_at(xh * 8 + z)
+    bi_own[...] = lax.dot_general(
+        chosen(128, 128, 0, 128), bin_[pl.ds(pl.multiple_of(quarter * 512, 512), 512)], NT,
+        preferred_element_type=f32,
+    ).astype(bf16)
+
+    def side_lanes(side):
+        return pl.ds(pl.multiple_of(side * 128, 128), 128)
+
+    def f_at(at, side):
+        return f.at[c, at, :, side_lanes(side)]
 
     def bm_at(q):
         return bm.at[lax.div(q, 2), lax.rem(q, 2)]
@@ -235,7 +256,7 @@
     qi[y, xl, c] = jnp.dot(ql[...], bin_[...], preferred_element_type=f32).astype(bf16)
     q_swap = copies.start(qi.at[y, xl, c], qi.at[y, xl, c], pair_l)
     f_in[...] = jnp.dot(li[...], bin_[...], preferred_element_type=f32).astype(bf16)
-    f_wait = permute(copies, local.at[2], f_in, f.at[c, z, xh], f_to, f_same)
+    f_wait = permute(copies, local.at[2], f_in, f_at(z, xh), f_to, f_same)
 
     forwards = []
 
@@ -248,7 +269,6 @@
     def around(slot, sign, first=None):
         return gather_stream(copies, y, along_y, sign, slot, pass_on(slot), first)
 
-    own_bi.wait()
     q_swap.wait_recv()
     g_wait()
     t_wait()
@@ -280,26 +300,26 @@
         around(lambda at: qi.at[at, 1, c], -1),
         over_x(),
         gather_stream(
-            copies, z, along_z, 1, lambda at: bi_at(quarter, xh * 8 + at).at[pl.ds(0, 256)]
+            copies, z, along_z, 1, lambda at: bi_at(xh * 8 + at, 0, 64)
         ),
         gather_stream(
-            copies, z, along_z, -1, lambda at: bi_at(quarter, xh * 8 + at).at[pl.ds(256, 256)]
+            copies, z, along_z, -1, lambda at: bi_at(xh * 8 + at, 64, 64)
         ),
     )
 
-    def quarter_at(q, low=0, count=512):
-        lanes = pl.ds(pl.multiple_of(lax.div(q, 2) * 1024, 1024), 1024)
-        return bia.at[lax.rem(q, 2) * 2 + c, pl.ds(low, count), lanes]
+    def quarter_at(q, low=0, count=1024):
+        start = pl.multiple_of(lax.div(q, 2) * 1024 + low, 512)
+        return bia.at[lax.rem(q, 2) * 2 + c, pl.ds(start, count)]
 
     x_l, x_r, x_f = lax.rem(x + 3, 4), lax.rem(x + 1, 4), lax.rem(x + 2, 4)
     i_right = copies.start(quarter_at(x), quarter_at(x), right)
     i_left = copies.start(quarter_at(x), quarter_at(x), left)
     i_core = [copies.start(quarter_at(x), quarter_at(x), other)]
 
-    for h in range(2):
-        bo[h] = jnp.zeros((PAD, PAD), bf16)
-        bo[h, :, pl.ds(0, COL)] = jnp.dot(
-            chosen(PAD, 2 * COL, h * COL, COL), bout[...], preferred_element_type=f32
+    bo[...] = jnp.zeros_like(bo)
+    for row, half in ((0, c), (PAD, 1 - c)):
+        bo[pl.ds(row, PAD), pl.ds(0, COL)] = jnp.dot(
+            chosen(PAD, 2 * COL, half * COL, COL), bout[...], preferred_element_type=f32
         ).astype(bf16)
     for copy in forwards + far:
         copy.wait_recv()
@@ -312,33 +332,39 @@
         btt[b] = lax.dot_general(bt[b], eye, TN, preferred_element_type=f32).astype(bf16)
 
     f_wait()
-    f_swap = copies.start(f.at[c, y, xl], f.at[c, y, xl], pair_l)
+    f_swap = copies.start(f_at(y, xl), f_at(y, xl), pair_l)
+
+    def fit_make(off):
+        d = turn(z, off)
+        value = lax.dot_general(
+            bm[0].reshape(2 * PAD, MAIN), gm[0, d], NT, preferred_element_type=f32
+        )
+        value += lax.dot_general(
+            bm[1].reshape(2 * PAD, MAIN), gm[1, d], NT, preferred_element_type=f32
+        )
+        tail = jnp.dot(btt[...].reshape(2 * PAD, 32), gt[d], preferred_element_type=f32)
+        fit_v[off] = value + tail[:, :TOK]
+
+    fit_ahead = Ahead(fit_make, 0)
 
     def fit_stream(b, part):
         low, count = PARTS[part]
 
-        def chunk(d, by):
-            value = lax.dot_general(
-                bm[0, b, pl.ds(low, count)], gm[0, d], NT, preferred_element_type=f32
-            )
-            value += lax.dot_general(
-                bm[1, b, pl.ds(low, count)], gm[1, d], NT, preferred_element_type=f32
-            )
-            tail = jnp.dot(btt[b, pl.ds(low, count)], gt[d], preferred_element_type=f32)
-            return value + tail[:, :TOK]
+        def chunk(off):
+            return fit_v[fit_ahead.need(off), pl.ds(b * PAD + low, count)]
 
         def done(total):
             stage[b, pl.ds(low, count)] = total.astype(bf16)
 
         return scatter_stream(
-            copies, z, along_z, 1 - 2 * b, chunk,
+            copies, along_z, 1 - 2 * b, chunk,
             fit_s.at[b, :, pl.ds(low, count)], fit_g.at[b, :, pl.ds(low, count)], done,
         )
 
     run(
         fit_stream(0, 0), fit_stream(1, 0), fit_stream(0, 1), fit_stream(1, 1),
-        around(lambda at: f.at[c, at, xl], 1),
-        around(lambda at: f.at[c, at, 1 - xl], -1, f_swap.wait_recv),
+        around(lambda at: f_at(at, xl), 1),
+        around(lambda at: f_at(at, 1 - xl), -1, f_swap.wait_recv),
     )
     swap = copies.start(stage.at[1 - xl], landed, pair_l)
     rot[xl] = stage[xl]
@@ -357,9 +383,9 @@
         for _ in range(3):
             yield
         i_right.wait_recv()
-        i_far.append(copies.start(quarter_at(x_l, 0, 256), quarter_at(x_l, 0, 256), right))
+        i_far.append(copies.start(quarter_at(x_l, 0, 512), quarter_at(x_l, 0, 512), right))
         i_left.wait_recv()
-        i_far.append(copies.start(quarter_at(x_r, 256, 256), quarter_at(x_r, 256, 256), left))
+        i_far.append(copies.start(quarter_at(x_r, 512, 512), quarter_at(x_r, 512, 512), left))
         for q in (x_l, x_r):
             i_core.append(copies.start(quarter_at(q), quarter_at(q), other))
 
@@ -372,20 +398,20 @@
 
     swaps, sums = {}, {}
 
+    def square_make(off):
+        d = turn(z, off)
+        first = jnp.dot(rot[0, :, pl.ds(0, SEQ)], f[0, d], preferred_element_type=f32)
+        second = jnp.dot(rot[1, :, pl.ds(0, SEQ)], f[1, d], preferred_element_type=f32)
+        pair_v[off] = first * first + second * second
+
+    square_ahead = Ahead(square_make, 1)
+
     def square_stream(near, part):
         low, count = PARTS[part]
         side = xh if near else 1 - xh
 
-        def chunk(d, by):
-            first = jnp.dot(
-                rot[0, pl.ds(low, count), pl.ds(0, SEQ)], f[0, d, side],
-                preferred_element_type=f32,
-            )
-            second = jnp.dot(
-                rot[1, pl.ds(low, count), pl.ds(0, SEQ)], f[1, d, side],
-                preferred_element_type=f32,
-            )
-            return first * first + second * second
+        def chunk(off):
+            return pair_v[square_ahead.need(off), pl.ds(low, count), side_lanes(side)]
 
         def done(total):
             if near:
@@ -396,7 +422,7 @@
                 swaps[part] = copies.start(half, landed_a.at[pl.ds(low, count)], pair_h)
 
         return scatter_stream(
-            copies, z, along_z, -1 if near else 1, chunk,
+            copies, along_z, -1 if near else 1, chunk,
             sq_s.at[near, :, pl.ds(low, count)], sq_g.at[near, :, pl.ds(low, count)], done,
         )
 
@@ -437,44 +463,43 @@
         copy.wait_recv()
 
     def image(group, carry):
-        value = lax.dot_general(s_buf[...], bia[group], NT, preferred_element_type=f32)
-        for j in range(4):
-            img[group * 4 + j] = value[:, j * 128 : (j + 1) * 128].astype(bf16)
+        value = jnp.dot(s_buf[...], bia[group], preferred_element_type=f32)
+        img[group * 2] = value[:, :256].astype(bf16)
+        img[group * 2 + 1] = value[:, 256:].astype(bf16)
         return carry
 
     lax.fori_loop(0, 4, image, 0)
 
-    def across(d, side):
+    def across(d):
         return pltpu.make_async_remote_copy(
-            src_ref=core_s.at[d, side], dst_ref=core_r.at[d, side],
-            send_sem=core_send.at[d, side], recv_sem=core_recv.at[d, side],
+            src_ref=core_s.at[d], dst_ref=core_r.at[d],
+            send_sem=core_send.at[d], recv_sem=core_recv.at[d],
             device_id=other, device_id_type=pl.DeviceIdType.MESH,
         )
 
-    for by in (4, -3, 3, -2, 2, -1, 1, 0):
-        d = turn(y, by)
-        for side in range(2):
-            core_s[d, side] = jnp.dot(
-                bo[1 - c], img[2 * d + side], preferred_element_type=f32
-            ).astype(bf16)
-            copy = across(d, side)
-            copy.start()
-            copies.started.append(copy)
-
+    def u_make(off):
+        d = turn(y, off)
+        value = jnp.dot(bo[...], img[d], preferred_element_type=f32)
+        pair_v[off] = value[:PAD]
+        core_s[d] = value[PAD:].astype(bf16)
+        copy = across(d)
+        copy.start()
+        copies.started.append(copy)
+
+    u_ahead = Ahead(u_make, 3)
     swaps, sums, seen = {}, {}, set()
 
     def u_stream(near, part):
         low, count = PARTS[part]
         side = xl if near else 1 - xl
 
-        def chunk(d, by):
-            value = jnp.dot(
-                bo[c, pl.ds(low, count)], img[2 * d + side], preferred_element_type=f32
-            )
-            if (near, by) not in seen:
-                seen.add((near, by))
-                across(d, side).wait_recv()
-            return value + core_r[d, side, pl.ds(low, count)].astype(f32)
+        def chunk(off):
+            key, d = u_ahead.need(off), turn(y, off)
+            if key not in seen:
+                seen.add(key)
+                across(d).wait_recv()
+            mine = pair_v[key, pl.ds(low, count), side_lanes(side)]
+            return mine + core_r[d, pl.ds(low, count), side_lanes(side)].astype(f32)
 
         def done(total):
             if near:
@@ -485,7 +510,7 @@
                 swaps[part] = copies.start(half, landed_b.at[pl.ds(low, count)], pair_l)
 
         return scatter_stream(
-            copies, y, along_y, -1 if near else 1, chunk,
+            copies, along_y, -1 if near else 1, chunk,
             u_s.at[near, :, pl.ds(low, count)], u_g.at[near, :, pl.ds(low, count)], done,
         )
 
@@ -527,12 +552,12 @@
             ram(16, 256),
             ram(SEQ, 128),
             ram(256, 128),
-            ram(2, PAD, PAD),
-            ram(4, 512, 2048),
-            ram(16, PAD, 128),
+            ram(2 * PAD, PAD),
+            ram(4, 2048, 512),
+            ram(RING, PAD, 256),
             ram(2, RING, TOK, MAIN),
             ram(RING, 32, 256),
-            ram(2, RING, 2, SEQ, 128),
+            ram(2, RING, SEQ, 256),
             ram(RING, 2, 2, 16, 128),
             ram(2, 2, PAD, MAIN),
             ram(2, 32, PAD),
@@ -546,8 +571,8 @@
             ram(PAD, 128),
             ram(PAD, 128),
             ram(PAD, 2048),
-            ram(RING, 2, PAD, 128),
-            ram(RING, 2, PAD, 128),
+            ram(RING, PAD, 256),
+            ram(RING, PAD, 256),
             *ring((2,), PAD, 128),
             ram(PAD, 128),
             ram(PAD, 128),
@@ -555,9 +580,11 @@
             ram(PAD, 128),
             dma((N_SEM,)),
             dma((N_SEM,)),
-            dma((RING, 2)),
-            dma((RING, 2)),
+            dma((RING,)),
+            dma((RING,)),
             dma((6,)),
+            pltpu.VMEM((RING, 2 * PAD, TOK), f32),
+            pltpu.VMEM((RING, PAD, 256), f32),
         ],
         compiler_params=pltpu.CompilerParams(
             collective_id=0, has_side_effects=True, vmem_limit_bytes=56 * 2**20

time: 172 us -> 167 us (0.971)
  the two profiles are of different devices: /device:TPU:2 before, /device:TPU:58 now
where the time goes in v5:
time: 167 us
  Pallas kernels  162 us (97%)
  local copies, waits for them, and re-layouts  4.15 us (2%)
    pallas_call x1, Pallas kernels, per_device(): pl.pallas_call(kernel, out_shape=[shape((COL, 128), f32), shape((COL, 128...  162 us
    unnamed x5, local copies, waits for them, and re-layouts  4.15 us

profile of v5, /device:TPU:58, one launch (start us, length us, event | category | flops | bytes accessed | tf_op | source)
XLA Modules:
  0.0 167.3 jit_solution(4842254182758098891)
XLA Ops:
  0.6 1.9 %copy.8.bout = bf16[516,258]{1,0:T(8,128)(2,1)} copy(bf16[516,258]{0,1:T(8,128)(2,1)} %param.10) | data formatting | bytes 532512 | tf_op args[4]
  2.5 162.5 %shard_map.77 = (f32[258,128]{1,0:T(8,128)}, bf16[258,128]{1,0:T(8,128)(2,1)}) custom-call(bf16[192,516]{1,0:T(8,128)(2,1)} %og.1, bf16[192,2048]{1,0:T(8,128)(2,1)} %li.1, bf16[16,516]{1,0:T(8,128)(2,1)} %qg.1, bf16[16,2048]{1,0:T(8,128)(2,1)} %ql.1, bf16[516,258]{1,0:T(8,128)(2,1)} %copy.8.bout, bf16[2048,128]{1,0:T(8,128)(2,1)} %bin_.1), custom_call_target="tpu_custom_call" | custom-call | tf_op jit(solution)/shard_map/pallas_call | solution.py:545
  165.0 0.0 copy-start
  165.0 1.6 copy.11
  166.6 0.0 copy-done
  166.6 0.6 copy.12
Async XLA Ops:
  165.0 1.6 copy-start

commit v6 on v5

--- a/solution.py
+++ b/solution.py
@@ -269,7 +269,6 @@
     def around(slot, sign, first=None):
         return gather_stream(copies, y, along_y, sign, slot, pass_on(slot), first)
 
-    q_swap.wait_recv()
     g_wait()
     t_wait()
     m_right = copies.start(bm_at(x), bm_at(x), right)
@@ -296,8 +295,8 @@
         around(lambda at: gm.at[c, at, pl.ds(0, 112)], 1),
         around(lambda at: gm.at[c, at, pl.ds(112, 96)], -1),
         around(lambda at: gt.at[at, pl.ds(c * 16, 16)], 1),
-        around(lambda at: qi.at[at, 0, c], 1),
-        around(lambda at: qi.at[at, 1, c], -1),
+        around(lambda at: qi.at[at, xl, c], 1),
+        around(lambda at: qi.at[at, 1 - xl, c], -1, q_swap.wait_recv),
         over_x(),
         gather_stream(
             copies, z, along_z, 1, lambda at: bi_at(xh * 8 + at, 0, 64)
@@ -312,6 +311,8 @@
         return bia.at[lax.rem(q, 2) * 2 + c, pl.ds(start, count)]
 
     x_l, x_r, x_f = lax.rem(x + 3, 4), lax.rem(x + 1, 4), lax.rem(x + 2, 4)
+    f_wait()
+    f_swap = copies.start(f_at(y, xl), f_at(y, xl), pair_l)
     i_right = copies.start(quarter_at(x), quarter_at(x), right)
     i_left = copies.start(quarter_at(x), quarter_at(x), left)
     i_core = [copies.start(quarter_at(x), quarter_at(x), other)]
@@ -331,9 +332,6 @@
     for b in range(2):
         btt[b] = lax.dot_general(bt[b], eye, TN, preferred_element_type=f32).astype(bf16)
 
-    f_wait()
-    f_swap = copies.start(f_at(y, xl), f_at(y, xl), pair_l)
-
     def fit_make(off):
         d = turn(z, off)
         value = lax.dot_general(
@@ -347,18 +345,26 @@
 
     fit_ahead = Ahead(fit_make, 0)
 
-    def fit_stream(b, part):
+    fit_swaps = []
+
+    def fit_stream(near, part):
         low, count = PARTS[part]
+        row = pl.multiple_of((xl if near else 1 - xl) * PAD + low, 16)
 
         def chunk(off):
-            return fit_v[fit_ahead.need(off), pl.ds(b * PAD + low, count)]
+            return fit_v[fit_ahead.need(off), pl.ds(row, count)]
 
         def done(total):
-            stage[b, pl.ds(low, count)] = total.astype(bf16)
+            if near:
+                rot[xl, pl.ds(low, count)] = total.astype(bf16)
+            else:
+                half = stage.at[pl.ds(low, count)]
+                half[...] = total.astype(bf16)
+                fit_swaps.append(copies.start(half, landed.at[pl.ds(low, count)], pair_l))
 
         return scatter_stream(
-            copies, along_z, 1 - 2 * b, chunk,
-            fit_s.at[b, :, pl.ds(low, count)], fit_g.at[b, :, pl.ds(low, count)], done,
+            copies, along_z, -1 if near else 1, chunk,
+            fit_s.at[near, :, pl.ds(low, count)], fit_g.at[near, :, pl.ds(low, count)], done,
         )
 
     run(
@@ -366,9 +372,8 @@
         around(lambda at: f_at(at, xl), 1),
         around(lambda at: f_at(at, 1 - xl), -1, f_swap.wait_recv),
     )
-    swap = copies.start(stage.at[1 - xl], landed, pair_l)
-    rot[xl] = stage[xl]
-    swap.wait_recv()
+    for swap in fit_swaps:
+        swap.wait_recv()
     rot[1 - xl] = landed[...]
     for h in range(2):
         qr[z, xh, h] = lax.dot_general(
@@ -563,7 +568,7 @@
             ram(2, 32, PAD),
             ram(2, PAD, 32),
             *ring((2,), PAD, TOK),
-            ram(2, PAD, TOK),
+            ram(PAD, TOK),
             ram(PAD, TOK),
             ram(2, PAD, TOK),
             ram(RING, 2, 2, 16, PAD),

time: 167 us -> 158 us (0.946)
  the two profiles are of different devices: /device:TPU:58 before, /device:TPU:12 now
where the time goes in v6:
time: 158 us
  Pallas kernels  153 us (97%)
  local copies, waits for them, and re-layouts  4.15 us (3%)
    pallas_call x1, Pallas kernels, per_device(): pl.pallas_call(kernel, out_shape=[shape((COL, 128), f32), shape((COL, 128...  153 us
    unnamed x5, local copies, waits for them, and re-layouts  4.15 us

profile of v6, /device:TPU:12, one launch (start us, length us, event | category | flops | bytes accessed | tf_op | source)
XLA Modules:
  0.0 157.7 jit_solution(6106066594314223377)
XLA Ops:
  0.6 1.9 %copy.8.bout = bf16[516,258]{1,0:T(8,128)(2,1)} copy(bf16[516,258]{0,1:T(8,128)(2,1)} %param.10) | data formatting | bytes 532512 | tf_op args[4]
  2.5 152.9 %shard_map.77 = (f32[258,128]{1,0:T(8,128)}, bf16[258,128]{1,0:T(8,128)(2,1)}) custom-call(bf16[192,516]{1,0:T(8,128)(2,1)} %og.1, bf16[192,2048]{1,0:T(8,128)(2,1)} %li.1, bf16[16,516]{1,0:T(8,128)(2,1)} %qg.1, bf16[16,2048]{1,0:T(8,128)(2,1)} %ql.1, bf16[516,258]{1,0:T(8,128)(2,1)} %copy.8.bout, bf16[2048,128]{1,0:T(8,128)(2,1)} %bin_.1), custom_call_target="tpu_custom_call" | custom-call | tf_op jit(solution)/shard_map/pallas_call | solution.py:550
  155.5 0.0 copy-start
  155.5 1.6 %copy.11 = f32[258,128]{1,0:T(8,128)} copy(f32[258,128]{1,0:T(8,128)} %get-tuple-element.4) | data formatting | bytes 264192
  157.1 0.0 copy-done
  157.1 0.6 copy.12
Async XLA Ops:
  155.5 1.6 %copy-start = (bf16[258,128]{1,0:T(8,128)(2,1)S(1)}, bf16[258,128]{1,0:T(8,128)(2,1)}, u32[]{:S(2)}) copy-start(bf16[258,128]{1,0:T(8,128)(2,1)} %get-tuple-element.5) | copy-start | bytes 198148
